TPU v7x, 32 devices: a whole 2x2x4 slice. The times are simulated.
32 devices in a mesh: img: 8 (over z, y), cap: 4 (over x, core).
Axes of the slice: x: 2, y: 2, z: 4, core: 2. Of those that a mesh axis runs over, the one named last changes fastest.
Arguments:
- tile_values: bfloat16 [5120, 512, 128], P('img', 'cap'), may hold values from -0.078125 to 0.078125
- tile_rows: int32 [8, 2560], P('img', 'cap'), may hold values from 0 to 63, as said below
- tile_cols: int32 [8, 2560], P('img', 'cap'), may hold values from 0 to 63
- tile_count: int32 [8, 4], P('img', 'cap'), may hold values from 81 to 640, as said below
- row_degree: float32 [65536], P('img'), may hold values from 1 to 10
- col_degree: float32 [32768], P('cap'), may hold values from 1 to 10
- start_panel: bfloat16 [32768, 128], P('cap'), may hold values from -6 to 6
Outputs:
- basis: float32 [65536, 128], P(('img', 'cap'))
- factor: float32 [128, 128], replicated
- next_panel: bfloat16 [32768, 128], P('cap')
Inputs may be any that keep to these rules, and one draw needn't show every extreme that they name: `tile_rows`: tile rows lie in 0 to 63; within one device's slots no (tile row, tile column) pair repeats. Only the first tile_count slots of a device are live; some device has all 640 slots live.
All inputs are finite; a program needn't handle non-finite values.
Results may differ from a plain program's by a relative error of at most 0.007.
Values may be sent and summed in bfloat16 or wider, within the bound.
No kernel may reach another device: no remote copies, remote signals or barrier semaphores. Data moves between devices by JAX's collectives and lax.ppermute only.
A program may use at most 256 MiB of HBM per device.

v0:
```python
import math

import jax
import jax.numpy as jnp
from jax import lax
from jax.sharding import PartitionSpec as P


def slot_select(indices, count, groups):
    slots = indices.shape[0]
    live = jnp.arange(slots, dtype=jnp.int32) < count
    return (
        (indices[None, :] == jnp.arange(groups, dtype=jnp.int32)[:, None]) & live[None, :]
    ).astype(jnp.float32)


def body(tile_values, tile_rows, tile_cols, tile_count, row_degree, col_degree, start_panel):
    slots, tile_size, _ = tile_values.shape
    width = start_panel.shape[1]
    row_total = row_degree.shape[0]
    col_total = col_degree.shape[0]
    row_groups = row_total // tile_size
    col_groups = col_total // tile_size
    rows = tile_rows[0]
    cols = tile_cols[0]
    count = tile_count[0, 0]
    row_scale = 1.0 / jnp.sqrt(row_degree)
    col_scale = 1.0 / jnp.sqrt(col_degree)
    caption_parts = lax.axis_size("cap")
    image_parts = lax.axis_size("img")
    root = math.sqrt(row_total * image_parts)
    scaled_start = (start_panel.astype(jnp.float32) * col_scale[:, None]).astype(jnp.bfloat16)
    gathered = scaled_start.reshape(col_groups, tile_size, width)[cols]
    product = jnp.einsum("tbc,tck->tbk", tile_values, gathered, preferred_element_type=jnp.float32)
    row_select = slot_select(rows, count, row_groups)
    image_terms = jnp.dot(
        row_select,
        product.reshape(slots, tile_size * width),
        precision=lax.Precision.HIGHEST,
        preferred_element_type=jnp.float32,
    ).reshape(row_total, width)
    share_rows = row_total // caption_parts
    share_start = lax.axis_index("cap") * share_rows
    image_panel = lax.psum(image_terms, "cap") * row_scale[:, None]
    gram = lax.psum(
        jnp.dot(
            image_panel.T,
            image_panel,
            precision=lax.Precision.HIGHEST,
            preferred_element_type=jnp.float32,
        ).astype(jnp.bfloat16),
        "img",
    ).astype(jnp.float32)
    lower = jnp.linalg.cholesky(gram)
    own_rows = lax.dynamic_slice_in_dim(image_panel, share_start, share_rows, 0)
    scaled_image = (image_panel * row_scale[:, None]).astype(jnp.bfloat16)
    basis = (
        lax.linalg.triangular_solve(lower, own_rows, left_side=False, lower=True, transpose_a=True)
        * root
    )
    factor = lower.T / root
    picked = scaled_image.reshape(row_groups, tile_size, width)[rows]
    transposed = jnp.einsum("tbc,tbk->tck", tile_values, picked, preferred_element_type=jnp.float32)
    col_select = slot_select(cols, count, col_groups)
    caption_terms = jnp.dot(
        col_select,
        transposed.reshape(slots, tile_size * width),
        precision=lax.Precision.HIGHEST,
        preferred_element_type=jnp.float32,
    ).reshape(col_total, width)
    caption_sums = lax.psum(caption_terms, "img")
    next_panel = (caption_sums * col_scale[:, None]).astype(jnp.bfloat16)
    return (basis, factor, next_panel)


def solution(mesh):
    placed = (
        P("img", "cap", None),
        P("img", "cap"),
        P("img", "cap"),
        P("img", "cap"),
        P("img"),
        P("cap"),
        P("cap", None),
    )
    return jax.shard_map(
        body,
        mesh=mesh,
        in_specs=placed,
        out_specs=(P(("img", "cap"), None), P(), P("cap", None)),
        check_vma=False,
    )
```

profile of v0, /device:TPU:0, one launch (start us, length us, event | category | flops | bytes accessed | tf_op | source)
XLA Modules:
  0.0 520.1 jit_solution(7480508575940463218)
XLA Ops:
  7.2 0.0 all-reduce.3.cloned.1.call-start
  7.2 0.8 sqrt.6
  8.0 0.7 fusion.13
  8.7 2.5 multiply_convert_fusion.2
  11.2 16.5 %gather_fusion = bf16[640,128,128]{2,1,0:T(8,128)(2,1)} fusion(bf16[64,128,128]{2,1,0:T(8,128)(2,1)S(1)} %bitcast.34, s32[1024]{0:T(1024)S(1)} %pad_clamp_fusion.1), kind=kCustom, calls=%fused_computation | custom fusion | bytes 41945600 | tf_op jit(solution)/shard_map/gather | solution.py:33
  27.7 30.6 %convolution_bitcast_fusion.1 = f32[640,128,128]{1,2,0:T(8,128)} fusion(bf16[640,128,128]{2,1,0:T(8,128)(2,1)} %gather_fusion, bf16[640,128,128]{2,1,0:T(8,128)(2,1)} %param.7), kind=kOutput, calls=%fused_computation.3 | convolution fusion | flops 2684354560 | bytes 83886080 | tf_op jit(solution)/shard_map/tbc,tck->tbk/dot_general | solution.py:34
  58.3 44.1 %copy.14 = f32[640,128,128]{0,2,1:T(8,128)} copy(f32[640,128,128]{1,2,0:T(8,128)} %convolution_bitcast_fusion.1) | data formatting | bytes 83886080 | tf_op jit(solution)/shard_map/tbc,tck->tbk/dot_general | solution.py:34
  103.1 29.9 %fusion.2 = f32[64,16384]{1,0:T(8,128)} fusion(f32[640,16384]{0,1:T(8,128)} %bitcast.35, s32[640]{0:T(1024)S(1)} %reduce.6, pred[640]{0:T(1024)(128)(4,1)S(1)} %iota_compare_fusion.4), kind=kOutput, calls=%fused_computation.14 | convolution fusion | flops 8053145600 | bytes 46140544 | tf_op jit(solution)/shard_map/dot_general | solution.py:36
  133.0 4.9 reshape.97
  137.9 0.0 all-reduce.3.cloned.1.call-update
  137.9 0.2 all-reduce.5.cloned.1.call-start
  138.2 0.4 copy-done.3
  138.6 0.1 copy-done.2
  138.7 87.6 %all-reduce.3.cloned.1.call-done = f32[8192,128]{1,0:T(8,128)} async-done(((f32[8192,128]{1,0:T(8,128)}), f32[8192,128]{1,0:T(8,128)}) %all-reduce.3.cloned.1.call-update) | async-done | bytes 4194320 | tf_op jit(solution)/shard_map/psum | solution.py:44
  226.3 4.2 multiply_convert_fusion.1
  230.5 16.6 %gather_fusion.1 = bf16[640,128,128]{2,1,0:T(8,128)(2,1)} fusion(bf16[64,128,128]{2,1,0:T(8,128)(2,1)S(1)} %bitcast.33, s32[1024]{0:T(1024)S(1)} %pad_clamp_fusion), kind=kCustom, calls=%fused_computation.1 | custom fusion | bytes 41945600 | tf_op jit(solution)/shard_map/gather | solution.py:62
  247.0 26.4 %convolution_bitcast_fusion = f32[640,128,128]{1,2,0:T(8,128)} fusion(bf16[640,128,128]{2,1,0:T(8,128)(2,1)} %gather_fusion.1, bf16[640,128,128]{2,1,0:T(8,128)(2,1)} %param.7), kind=kOutput, calls=%fused_computation.2 | convolution fusion | flops 2684354560 | bytes 83886080 | tf_op jit(solution)/shard_map/tbc,tbk->tck/dot_general | solution.py:63
  273.4 44.0 %copy.18 = f32[640,128,128]{0,2,1:T(8,128)} copy(f32[640,128,128]{1,2,0:T(8,128)} %convolution_bitcast_fusion) | data formatting | bytes 83886080 | tf_op jit(solution)/shard_map/tbc,tbk->tck/dot_general | solution.py:63
  317.4 29.9 %fusion.5 = f32[64,16384]{1,0:T(8,128)} fusion(f32[640,16384]{0,1:T(8,128)} %bitcast.36, s32[640]{0:T(1024)S(1)} %reduce.8, pred[640]{0:T(1024)(128)(4,1)S(1)} %iota_compare_fusion.4), kind=kOutput, calls=%fused_computation.16 | convolution fusion | flops 8053145600 | bytes 46140544 | tf_op jit(solution)/shard_map/dot_general | solution.py:65
  347.3 4.9 reshape.100
  352.2 0.0 all-reduce.5.cloned.1.call-update
  352.2 10.2 %convolution_convert_fusion = bf16[128,128]{0,1:T(8,128)(2,1)S(1)} fusion(f32[8192,128]{1,0:T(8,128)} %get-tuple-element.10), kind=kOutput, calls=%fused_computation.9 | convolution fusion | flops 1610629120 | bytes 4227072 | tf_op jit(solution)/shard_map/dot_general | solution.py:46
  362.4 39.4 %psum.22 = bf16[128,128]{0,1:T(8,128)(2,1)S(1)} all-reduce(bf16[128,128]{0,1:T(8,128)(2,1)S(1)} %convolution_convert_fusion), channel_id=1, replica_groups=mesh['img'=8,'cap'=4] {'img'}, use_global_device_ids=true, to_apply=%region_1.0 | all-reduce | flops 16384 | bytes 65536 | tf_op jit(solution)/shard_map/psum | solution.py:45
  401.9 0.1 copy.16
  402.0 11.7 %cholesky.16 = f32[128,128]{1,0:T(8,128)S(1)} custom-call(f32[128,128]{1,0:T(8,128)S(1)} %fusion.12), custom_call_target="Cholesky" | custom-call | tf_op jit(solution)/shard_map/jit(cholesky)/cholesky | solution.py:54
  413.7 0.6 compare_reduce_fusion
  414.4 0.7 multiply_bitcast_fusion
  415.0 9.8 %custom-call.6 = f32[1,128,128]{1,2,0:T(8,128)S(1)} custom-call(f32[1,128,128]{2,1,0:T(8,128)S(1)} %get-tuple-element.12), custom_call_target="InvertDiagBlocksLowerTriangular" | custom-call | tf_op jit(solution)/shard_map/triangular_solve | solution.py:58
  424.9 0.7 copy.19
  425.6 3.2 convolution_multiply_fusion
  428.8 80.7 %all-reduce.5.cloned.1.call-done = f32[8192,128]{1,0:T(8,128)} async-done(((f32[8192,128]{1,0:T(8,128)}), f32[8192,128]{1,0:T(8,128)}) %all-reduce.5.cloned.1.call-update) | async-done | bytes 4194320 | tf_op jit(solution)/shard_map/psum | solution.py:71
  509.5 3.8 multiply_convert_fusion
  (17 shorter events, 0.1 us)
Async XLA Ops:
  7.2 219.1 %all-reduce.3.cloned.1.call-start = ((), (), s32[]{:S(2)}) async-start(), calls=%async_computation | async-start | bytes 8388608 | tf_op jit(solution)/shard_map/psum | solution.py:44
  8.0 0.7 copy-start
  58.3 44.7 %copy-start.4 = (s32[1,640]{1,0:T(1,128)S(1)}, s32[1,640]{1,0:T(1,128)}, u32[]{:S(2)}) copy-start(s32[1,640]{1,0:T(1,128)} %param.8) | copy-start | bytes 7684
  137.9 0.7 copy-start.3
  137.9 0.8 copy-start.2
  137.9 371.5 %all-reduce.5.cloned.1.call-start = ((), (), s32[]{:S(2)}) async-start(), calls=%async_computation.1 | async-start | bytes 8388608 | tf_op jit(solution)/shard_map/psum | solution.py:71
  352.2 157.3 %copy-start.1 = (f32[8192]{0:T(1024)S(1)}, f32[8192]{0:T(1024)}, u32[]{:S(2)}) copy-start(f32[8192]{0:T(1024)} %copy-done) | copy-start | bytes 98308
Sparse Core Ops, SparseCore 0:
  138.1 88.1 all-reduce.2
  352.3 157.1 all-reduce.4
where the time goes:
time: 522 us; the launch traced here: 520 us
  waiting for transfers between devices  168 us (32%)
  local copies, waits for them, and re-layouts  133 us (25%)
  matrix products  130 us (25%)
  blocking collectives  39.4 us (8%)
  other arithmetic  34.1 us (7%)
  between operations  14.8 us (3%)
    psum x1, waiting for transfers between devices, body(): image_panel = lax.psum(image_terms, 'cap') * row_scale[:, None]  87.6 us
    psum x1, waiting for transfers between devices, body(): caption_sums = lax.psum(caption_terms, 'img')  80.7 us
    dot_general x1, local copies, waits for them, and re-layouts, body(): jnp.einsum('tbc,tck->tbk', tile_values, gathered, preferred_element_type=...  44.1 us
    dot_general x1, local copies, waits for them, and re-layouts, body(): jnp.einsum('tbc,tbk->tck', tile_values, picked, preferred_element_type=jn...  44 us
    psum x1, blocking collectives, body(): lax.psum(jnp.dot(image_panel.T, image_panel, precision=lax.Precision.HIGH...  39.4 us
    dot_general x1, matrix products, body(): jnp.einsum('tbc,tck->tbk', tile_values, gathered, preferred_element_type=...  30.6 us
    dot_general x1, matrix products, body(): jnp.dot(row_select, product.reshape(slots, tile_size * width), precision=...  29.9 us
    dot_general x1, matrix products, body(): jnp.dot(col_select, transposed.reshape(slots, tile_size * width), precisi...  29.9 us
  transfers between devices with their start and end apart: 2, of which 2 were waited for; matrix products, arithmetic and copies ran while one was open for 7% of the time, Pallas kernels for 0%

commit v1 on v0

v1 whole, which is shorter than its diff:
```python
import functools
import math

import jax
import jax.numpy as jnp
from jax import lax
from jax.experimental import pallas as pl
from jax.experimental.pallas import tpu as pltpu
from jax.sharding import PartitionSpec as P

F32 = jnp.float32
BF16 = jnp.bfloat16


def swap(x, axis, bit):
    n = lax.axis_size(axis)
    return lax.ppermute(x, axis, [(i, i ^ (1 << bit)) for i in range(n)])


def bit_of(axis, bit):
    return (lax.axis_index(axis) >> bit) & 1


def accumulate(transposed, step, unroll, count, src, dst, tiles, panel, accs):
    g = pl.program_id(0)
    dead = accs[0].shape[0] - 1

    @pl.when(g == 0)
    def _():
        for acc in accs:
            acc[...] = jnp.zeros_like(acc)

    dims = (((0,), (0,)), ((), ())) if transposed else (((1,), (0,)), ((), ()))

    def group(u, carry):
        for j in range(unroll):
            t = u * unroll + j
            s = g * step + t
            to = jnp.where(s < count, dst[s], dead)
            accs[j % len(accs)][to] += lax.dot_general(
                tiles[t], panel[src[s]], dims, preferred_element_type=F32
            )
        return carry

    groups = jnp.clip(pl.cdiv(count - g * step, unroll), 0, step // unroll)
    lax.fori_loop(0, groups, group, 0)


def total(accs, at):
    value = accs[0][at]
    for acc in accs[1:]:
        value = value + acc[at]
    return value


def forward_kernel(step, unroll, src, dst, meta, tiles, panel, own, send, *accs):
    accumulate(False, step, unroll, meta[0], src, dst, tiles, panel, accs)

    @pl.when(pl.program_id(0) == pl.num_programs(0) - 1)
    def _():
        core = meta[1]
        shares, share = own.shape[0], own.shape[1]
        for h in range(shares):

            def block(i, carry):
                own[h, i] = total(accs, (2 * h + core) * share + i)
                send[h, i] = total(accs, (2 * h + 1 - core) * share + i).astype(BF16)
                return carry

            lax.fori_loop(0, share, block, 0)


def backward_kernel(
    step, unroll, src, dst, meta, tiles, first, second, own_a, send_a, own_b, send_b, panel, sem, *accs
):
    half = panel.shape[0] // 2

    @pl.when(pl.program_id(0) == 0)
    def _():
        one = pltpu.make_async_copy(first, panel.at[pl.ds(0, half)], sem.at[0])
        two = pltpu.make_async_copy(second, panel.at[pl.ds(half, half)], sem.at[1])
        one.start()
        two.start()
        one.wait()
        two.wait()

    accumulate(True, step, unroll, meta[0], src, dst, tiles, panel, accs)

    @pl.when(pl.program_id(0) == pl.num_programs(0) - 1)
    def _():
        part = own_a.shape[0]
        for own, send, base, bit in ((own_a, send_a, 0, meta[1]), (own_b, send_b, 2 * part, meta[2])):

            def block(i, carry):
                own[i] = total(accs, base + bit * part + i)
                send[i] = total(accs, base + (1 - bit) * part + i).astype(BF16)
                return carry

            lax.fori_loop(0, part, block, 0)


STEP = 64
UNROLL = 32
SUMS = 4


def tile_spec(step, tile):
    def at(g, src, dst, meta):
        return (jnp.minimum(g, jnp.maximum((meta[0] - 1) // step, 0)), 0, 0)

    return pl.BlockSpec((step, tile, tile), at)


def whole(shape):
    return pl.BlockSpec(shape, lambda g, *_: (0,) * len(shape), pipeline_mode=pl.Buffered(1))


def forward(src, dst, meta, tiles, panel, shares):
    slots, tile, _ = tiles.shape
    groups, _, width = panel.shape
    shape = (shares // 2, groups // shares, tile, width)
    return pl.pallas_call(
        functools.partial(forward_kernel, STEP, UNROLL),
        grid_spec=pltpu.PrefetchScalarGridSpec(
            num_scalar_prefetch=3,
            grid=(slots // STEP,),
            in_specs=[tile_spec(STEP, tile), whole(panel.shape)],
            out_specs=[whole(shape), whole(shape)],
            scratch_shapes=[pltpu.VMEM((groups + 1, tile, width), F32)] * SUMS,
        ),
        out_shape=[jax.ShapeDtypeStruct(shape, F32), jax.ShapeDtypeStruct(shape, BF16)],
        compiler_params=pltpu.CompilerParams(
            vmem_limit_bytes=56 * 2**20, dimension_semantics=("arbitrary",)
        ),
        name="forward",
    )(src, dst, meta, tiles, panel)


def backward(src, dst, meta, tiles, first, second, groups):
    slots, tile, _ = tiles.shape
    half, _, width = first.shape
    shape = (groups // 4, tile, width)
    outs = [jax.ShapeDtypeStruct(shape, F32), jax.ShapeDtypeStruct(shape, BF16)]
    return pl.pallas_call(
        functools.partial(backward_kernel, STEP, UNROLL),
        grid_spec=pltpu.PrefetchScalarGridSpec(
            num_scalar_prefetch=3,
            grid=(slots // STEP,),
            in_specs=[
                tile_spec(STEP, tile),
                pl.BlockSpec(memory_space=pl.ANY),
                pl.BlockSpec(memory_space=pl.ANY),
            ],
            out_specs=[whole(shape)] * 4,
            scratch_shapes=[
                pltpu.VMEM((2 * half, tile, width), BF16),
                pltpu.SemaphoreType.DMA((2,)),
            ]
            + [pltpu.VMEM((groups + 1, tile, width), F32)] * SUMS,
        ),
        out_shape=outs * 2,
        compiler_params=pltpu.CompilerParams(
            vmem_limit_bytes=56 * 2**20, dimension_semantics=("arbitrary",)
        ),
        name="backward",
    )(src, dst, meta, tiles, first, second)


def halves(x, bit):
    n = x.shape[0] // 2
    return (
        lax.dynamic_slice_in_dim(x, bit * n, n, 0),
        lax.dynamic_slice_in_dim(x, (1 - bit) * n, n, 0),
    )


def joined(own, other, bit):
    return jnp.where(bit == 0, jnp.concatenate([own, other]), jnp.concatenate([other, own]))


def reduce_rest(own, arrived, bits):
    value = own + arrived.astype(F32)
    for bit in bits[1:-1]:
        keep, give = halves(value, bit_of("img", bit))
        value = keep + swap(give.astype(BF16), "img", bit).astype(F32)
    mine = value.astype(BF16)
    return mine.astype(F32) + swap(mine, "img", bits[-1]).astype(F32)


def scatter_start(x, bits):
    for bit in bits[:-1]:
        x = halves(x, bit_of("img", bit))[0]
    return x


def gather_back(x, bits):
    for bit in reversed(bits[:-1]):
        x = joined(x, swap(x, "img", bit), bit_of("img", bit))
    return x


def body(tile_values, tile_rows, tile_cols, tile_count, row_degree, col_degree, start_panel):
    slots, tile, _ = tile_values.shape
    width = start_panel.shape[1]
    row_total = row_degree.shape[0]
    col_total = col_degree.shape[0]
    row_groups = row_total // tile
    col_groups = col_total // tile
    rows = tile_rows[0]
    cols = tile_cols[0]
    count = tile_count[0, 0]
    caps = lax.axis_size("cap")
    imgs = lax.axis_size("img")
    cap_bits = caps.bit_length() - 1
    img_bits = imgs.bit_length() - 1
    core = bit_of("cap", 0)
    root = math.sqrt(row_total * imgs)
    share = row_groups // caps
    row_scale = (1.0 / jnp.sqrt(row_degree)).reshape(caps // 2, 2, share, tile, 1)
    col_scale = (1.0 / jnp.sqrt(col_degree)).reshape(col_groups, tile, 1)
    scaled_start = (start_panel.astype(F32).reshape(col_groups, tile, width) * col_scale).astype(BF16)

    own, send = forward(cols, rows, jnp.stack([count, core]), tile_values, scaled_start, caps)
    part = own + swap(send, "cap", 0).astype(F32)
    for bit in range(1, cap_bits):
        part = part + swap(part.astype(BF16), "cap", bit).astype(F32)
    own_scale = lax.dynamic_index_in_dim(row_scale, core, 1, False)
    image = part * own_scale
    scaled = (image * own_scale).astype(BF16).reshape(row_groups // 2, tile, width)
    other = swap(scaled, "cap", 0)

    block = rows // share
    place = ((block & 1) ^ core) * (row_groups // 2) + (block >> 1) * share + rows % share
    order_a = list(range(img_bits))
    order_b = order_a[1:] + order_a[:1]
    own_a, send_a, own_b, send_b = backward(
        place,
        cols,
        jnp.stack([count, bit_of("img", order_a[0]), bit_of("img", order_b[0])]),
        tile_values,
        scaled,
        other,
        col_groups,
    )
    scale_a, scale_b = col_scale[: col_groups // 2], col_scale[col_groups // 2 :]
    got_a = swap(send_a, "img", order_a[0])
    got_b = swap(send_b, "img", order_b[0])
    sum_a = reduce_rest(own_a, got_a, order_a)
    sum_b = reduce_rest(own_b, got_b, order_b)
    next_a = (sum_a * scatter_start(scale_a, order_a)).astype(BF16)
    next_b = (sum_b * scatter_start(scale_b, order_b)).astype(BF16)
    next_panel = jnp.concatenate(
        [gather_back(next_a, order_a), gather_back(next_b, order_b)]
    ).reshape(col_total, width)

    mine = lax.dynamic_index_in_dim(image, lax.axis_index("cap") >> 1, 0, False).reshape(
        share * tile, width
    )
    gram = jnp.dot(mine.T, mine, precision=lax.Precision.HIGHEST, preferred_element_type=F32)
    for axis, bits in (("cap", cap_bits), ("img", img_bits)):
        for bit in range(bits):
            gram = gram + swap(gram, axis, bit)
    lower = jnp.linalg.cholesky(gram)
    basis = (
        lax.linalg.triangular_solve(lower, mine, left_side=False, lower=True, transpose_a=True) * root
    )
    factor = lower.T / root
    return (basis, factor, next_panel)


def solution(mesh):
    placed = (
        P("img", "cap", None),
        P("img", "cap"),
        P("img", "cap"),
        P("img", "cap"),
        P("img"),
        P("cap"),
        P("cap", None),
    )
    return jax.shard_map(
        body,
        mesh=mesh,
        in_specs=placed,
        out_specs=(P(("img", "cap"), None), P(), P("cap", None)),
        check_vma=False,
    )
```

time: 522 us -> 170 us (0.33)
  local copies, waits for them, and re-layouts: 133 us -> 6.22 us
  matrix products: 130 us -> 3.76 us
  waiting for transfers between devices: 168 us -> 56.4 us
  blocking collectives: 39.4 us -> 0 us
  starting transfers between devices: 0.26 us -> 29.3 us
  Pallas kernels: 0 us -> 27.4 us
  between operations: 14.8 us -> 1.56 us
  other arithmetic: 34.1 us -> 43.9 us
    psum x2 -> x0, waiting for transfers between devices: 168 us -> none  [the longest x1 87.6 us: body(): image_panel = lax.psum(image_terms, 'cap') * row_scale[:, None]]
    dot_general x5 -> x1, matrix products: 127 us -> 1.82 us  [body(): jnp.dot(mine.T, mine, precision=lax.Precision.HIGHEST, preferred_element_...]
    dot_general x2 -> x0, local copies, waits for them, and re-layouts: 88.1 us -> none  [the longest x1 44.1 us: body(): jnp.einsum('tbc,tck->tbk', tile_values, gathered, preferred_element_type=...]
    ppermute x0 -> x18, waiting for transfers between devices: none -> 56.4 us  [swap(): return lax.ppermute(x, axis, [(i, i ^ 1 << bit) for i in range(n)])]
    psum x1 -> x0, blocking collectives: 39.4 us -> none  [body(): lax.psum(jnp.dot(image_panel.T, image_panel, precision=lax.Precision.HIGH...]
    gather x2 -> x0, local copies, waits for them, and re-layouts: 33.1 us -> none  [the longest x1 16.6 us: body(): picked = scaled_image.reshape(row_groups, tile_size, width)[rows]]
    ppermute x0 -> x18, starting transfers between devices: none -> 29.3 us  [swap(): return lax.ppermute(x, axis, [(i, i ^ 1 << bit) for i in range(n)])]
    pallas_call x0 -> x2, Pallas kernels: none -> 27.4 us  [the longest x1 14.3 us: backward(): pl.pallas_call(functools.partial(backward_kernel, STEP, UNROLL), grid_spe...]
  transfers between devices with their start and end apart: 2 -> 18, of which waited for: 2 -> 12; matrix products, arithmetic and copies ran while one was open for 7% -> 22% of each run, Pallas kernels for 0% -> 0%
where the time goes in v1:
time: 170 us; the launch traced here: 169 us
  waiting for transfers between devices  56.4 us (33%)
  other arithmetic  43.9 us (26%)
  starting transfers between devices  29.3 us (17%)
  Pallas kernels  27.4 us (16%)
  local copies, waits for them, and re-layouts  6.22 us (4%)
  matrix products  3.76 us (2%)
    ppermute x18, waiting for transfers between devices, swap(): return lax.ppermute(x, axis, [(i, i ^ 1 << bit) for i in range(n)])  56.4 us
    ppermute x18, starting transfers between devices, swap(): return lax.ppermute(x, axis, [(i, i ^ 1 << bit) for i in range(n)])  29.3 us
    pallas_call x1, Pallas kernels, backward(): pl.pallas_call(functools.partial(backward_kernel, STEP, UNROLL), grid_spe...  14.3 us
    pallas_call x1, Pallas kernels, forward(): pl.pallas_call(functools.partial(forward_kernel, STEP, UNROLL), grid_spec...  13.1 us
    another operation x3, other arithmetic, body(): lower = jnp.linalg.cholesky(gram)  12.4 us
    another operation x1, other arithmetic, body(): lax.linalg.triangular_solve(lower, mine, left_side=False, lower=True, tra...  9.81 us
    convert_element_type x1, other arithmetic, body(): (start_panel.astype(F32).reshape(col_groups, tile, width) * col_scale).as...  3.43 us
  transfers between devices with their start and end apart: 18, of which 12 were waited for; matrix products, arithmetic and copies ran while one was open for 22% of the time, Pallas kernels for 0%

profile of v1, /device:TPU:0, one launch (start us, length us, event | category | flops | bytes accessed | tf_op | source)
XLA Modules:
  0.0 168.6 jit_solution(17858321335740566835)
XLA Ops:
  1.3 1.3 reduce.7.dst
  2.6 1.3 reduce.6.src.dst
  5.2 3.4 %fusion.panel = bf16[64,128,128]{2,1,0:T(8,128)(2,1)} fusion(bf16[64,128,128]{2,1,0:T(8,128)(2,1)} %bitcast.44, f32[64,128]{1,0:T(8,128)S(1)} %get-tuple-element.28), kind=kLoop, calls=%fused_computation.1 | loop fusion | flops 3145728 | bytes 4227072 | tf_op jit(solution)/shard_map/convert_element_type | solution.py:221
  8.6 13.1 %forward.1 = (f32[2,16,128,128]{3,2,1,0:T(8,128)}, bf16[2,16,128,128]{3,2,1,0:T(8,128)(2,1)}) custom-call(s32[640]{0:T(1024)} %reduce.6.src.dst, s32[640]{0:T(1024)} %reduce.7.dst, s32[2]{0:T(128)} %pad_add_fusion.meta, bf16[640,128,128]{2,1,0:T(8,128)(2,1)} %tiles.3, bf16[64,128,128]{2,1,0:T(8,128)(2,1)} %fusion.panel), custom_call_target="tpu_custom_call" | custom-call | tf_op jit(solution)/shard_map/forward/pallas_call | solution.py:122
  21.8 2.9 %collective-permute-done = bf16[2,16,128,128]{3,2,1,0:T(8,128)(2,1)S(1)} collective-permute-done((bf16[2,16,128,128]{3,2,1,0:T(8,128)(2,1)}, bf16[2,16,128,128]{3,2,1,0:T(8,128)(2,1)S(1)}, u32[]{:S(2)}, u32[]{:S(2)}) %collective-permute-start) | collective-permute-done | bytes 1048608 | tf_op jit(solution)/shard_map/ppermute | solution.py:17
  24.6 3.0 %fusion.1 = bf16[2,16,128,128]{3,2,1,0:T(8,128)(2,1)} fusion(f32[2,16,128,128]{3,2,1,0:T(8,128)} %get-tuple-element.9, bf16[2,16,128,128]{3,2,1,0:T(8,128)(2,1)S(1)} %collective-permute-done), kind=kLoop, calls=%fused_computation.7 | loop fusion | flops 1572864 | bytes 4194304 | tf_op jit(solution)/shard_map/convert_element_type | solution.py:226
  27.7 1.1 collective-permute-start.1
  28.8 24.4 %collective-permute-done.1 = bf16[2,16,128,128]{3,2,1,0:T(8,128)(2,1)} collective-permute-done((bf16[2,16,128,128]{3,2,1,0:T(8,128)(2,1)}, bf16[2,16,128,128]{3,2,1,0:T(8,128)(2,1)}, u32[]{:S(2)}, u32[]{:S(2)}) %collective-permute-start.1) | collective-permute-done | bytes 1048608 | tf_op jit(solution)/shard_map/ppermute | solution.py:17
  53.2 3.1 %multiply_convert_fusion = (bf16[2,16,128,128]{3,2,1,0:T(8,128)(2,1)}, f32[2,16,128,128]{3,2,1,0:T(8,128)}) fusion(f32[2,16,128]{2,1,0:T(8,128)S(1)} %dynamic-slice_bitcast_fusion, bf16[2,16,128,128]{3,2,1,0:T(8,128)(2,1)} %collective-permute-done.1, f32[2,16,128,128]{3,2,1,0:T(8,128)S(1)} %copy-done, bf16[2,16,128,128]{3,2,1,0:T(8,128)(2,1)S(1)} %collective-permute-done), kind=kLoop, calls=%fused_computation.4 | loop fusion | flops 3670016 | bytes 7356416 | tf_op jit(solution)/shard_map/convert_element_type | solution.py:229
  57.5 1.3 constant_dynamic-slice_fusion
  60.1 14.3 %backward.1 = (f32[16,128,128]{2,1,0:T(8,128)}, bf16[16,128,128]{2,1,0:T(8,128)(2,1)}, f32[16,128,128]{2,1,0:T(8,128)}, bf16[16,128,128]{2,1,0:T(8,128)(2,1)}) custom-call(s32[640]{0:T(1024)} %fusion.5.src, s32[640]{0:T(1024)} %reduce.6.src.dst, s32[3]{0:T(128)} %pad_add_fusion.1.meta, bf16[640,128,128]{2,1,0:T(8,128)(2,1)} %tiles.3, ...), custom_call_target="tpu_custom_call" | custom-call | tf_op jit(solution)/shard_map/backward/pallas_call | solution.py:144
  74.4 12.2 %collective-permute-start.13 = (bf16[16,128,128]{2,1,0:T(8,128)(2,1)}, bf16[16,128,128]{2,1,0:T(8,128)(2,1)S(1)}, u32[]{:S(2)}, u32[]{:S(2)}) collective-permute-start(bf16[16,128,128]{2,1,0:T(8,128)(2,1)} %get-tuple-element.14), channel_id=1, source_target_pairs={{0,8},{4,12},{8,0},{12,4},{16,24},{20,28},{24,16},{28,20},{1,9},{5... | collective-permute-start | bytes 1572872 | tf_op jit(solution)/shard_map/ppermute | solution.py:17
  86.6 1.8 %convolution_bitcast_fusion = f32[128,128]{0,1:T(8,128)S(1)} fusion(f32[1,16,128,128]{3,2,1,0:T(8,128)S(1)} %constant_dynamic-slice_fusion), kind=kOutput, calls=%fused_computation.8 | convolution fusion | flops 402653184 | bytes 1114112 | tf_op jit(solution)/shard_map/dot_general | solution.py:259
  88.5 1.2 collective-permute-done.2
  89.9 4.3 %collective-permute-done.3 = f32[128,128]{0,1:T(8,128)S(1)} collective-permute-done((f32[128,128]{0,1:T(8,128)S(1)}, f32[128,128]{0,1:T(8,128)S(1)}, u32[]{:S(2)}, u32[]{:S(2)}) %collective-permute-start.3) | collective-permute-done | bytes 65568 | tf_op jit(solution)/shard_map/ppermute | solution.py:17
  94.1 3.5 %collective-permute-start.4 = (f32[128,128]{0,1:T(8,128)S(1)}, f32[128,128]{0,1:T(8,128)S(1)}, u32[]{:S(2)}, u32[]{:S(2)}) collective-permute-start(f32[128,128]{0,1:T(8,128)S(1)} %add.102), channel_id=1, source_target_pairs={{0,4},{4,0},{8,12},{12,8},{16,20},{20,16},{24,28},{28,24},{1,5},{5... | collective-permute-start | bytes 196616 | tf_op jit(solution)/shard_map/ppermute | solution.py:17
  97.7 2.6 %collective-permute-done.4 = f32[128,128]{0,1:T(8,128)S(1)} collective-permute-done((f32[128,128]{0,1:T(8,128)S(1)}, f32[128,128]{0,1:T(8,128)S(1)}, u32[]{:S(2)}, u32[]{:S(2)}) %collective-permute-start.4) | collective-permute-done | bytes 65568 | tf_op jit(solution)/shard_map/ppermute | solution.py:17
  100.3 2.1 %collective-permute-start.5 = (f32[128,128]{0,1:T(8,128)S(1)}, f32[128,128]{0,1:T(8,128)S(1)}, u32[]{:S(2)}, u32[]{:S(2)}) collective-permute-start(f32[128,128]{0,1:T(8,128)S(1)} %add.103), channel_id=1, source_target_pairs={{0,8},{4,12},{8,0},{12,4},{16,24},{20,28},{24,16},{28,20},{1,9},{5... | collective-permute-start | bytes 196616 | tf_op jit(solution)/shard_map/ppermute | solution.py:17
  102.3 2.2 %collective-permute-done.5 = f32[128,128]{0,1:T(8,128)S(1)} collective-permute-done((f32[128,128]{0,1:T(8,128)S(1)}, f32[128,128]{0,1:T(8,128)S(1)}, u32[]{:S(2)}, u32[]{:S(2)}) %collective-permute-start.5) | collective-permute-done | bytes 65568 | tf_op jit(solution)/shard_map/ppermute | solution.py:17
  105.5 1.1 convert_add_fusion.1
  107.4 2.9 %collective-permute-start.14 = (bf16[8,128,128]{2,1,0:T(8,128)(2,1)}, bf16[8,128,128]{2,1,0:T(8,128)(2,1)}, u32[]{:S(2)}, u32[]{:S(2)}) collective-permute-start(bf16[8,128,128]{2,1,0:T(8,128)(2,1)} %dynamic-slice_convert_fusion), channel_id=1, source_target_pairs={{0,16},{4,20},{8,24},{12,28},{16,0},{20,4},{24,8},{28,12},{1,17},{... | collective-permute-start | bytes 786440 | tf_op jit(solution)/shard_map/ppermute | solution.py:17
  111.2 1.5 convert_add_fusion.2
  113.4 2.0 %collective-permute-start.9 = (bf16[8,128,128]{2,1,0:T(8,128)(2,1)}, bf16[8,128,128]{2,1,0:T(8,128)(2,1)}, u32[]{:S(2)}, u32[]{:S(2)}) collective-permute-start(bf16[8,128,128]{2,1,0:T(8,128)(2,1)} %dynamic-slice_convert_fusion.1), channel_id=1, source_target_pairs={{0,8},{4,12},{8,0},{12,4},{16,24},{20,28},{24,16},{28,20},{1,9},{5... | collective-permute-start | bytes 786440 | tf_op jit(solution)/shard_map/ppermute | solution.py:17
  115.5 6.0 %collective-permute-done.14 = bf16[8,128,128]{2,1,0:T(8,128)(2,1)} collective-permute-done((bf16[8,128,128]{2,1,0:T(8,128)(2,1)}, bf16[8,128,128]{2,1,0:T(8,128)(2,1)}, u32[]{:S(2)}, u32[]{:S(2)}) %collective-permute-start.14) | collective-permute-done | bytes 262176 | tf_op jit(solution)/shard_map/ppermute | solution.py:17
  122.5 2.1 %collective-permute-start.15 = (bf16[8,128,128]{2,1,0:T(8,128)(2,1)S(1)}, bf16[8,128,128]{2,1,0:T(8,128)(2,1)S(1)}, u32[]{:S(2)}, u32[]{:S(2)}) collective-permute-start(bf16[8,128,128]{2,1,0:T(8,128)(2,1)S(1)} %add_convert_fusion), channel_id=1, source_target_pairs={{0,4},{4,0},{8,12},{12,8},{16,20},{20,16},{24,28},{28,24},{1,5},{5... | collective-permute-start | bytes 786440 | tf_op jit(solution)/shard_map/ppermute | solution.py:17
  126.2 11.7 %cholesky.16 = f32[128,128]{1,0:T(8,128)S(1)} custom-call(f32[128,128]{1,0:T(8,128)S(1)} %fusion.4), custom_call_target="Cholesky" | custom-call | tf_op jit(solution)/shard_map/jit(cholesky)/cholesky | solution.py:263
  138.1 3.0 %collective-permute-start.16 = (bf16[8,128,128]{2,1,0:T(8,128)(2,1)S(1)}, bf16[8,128,128]{2,1,0:T(8,128)(2,1)S(1)}, u32[]{:S(2)}, u32[]{:S(2)}) collective-permute-start(bf16[8,128,128]{2,1,0:T(8,128)(2,1)S(1)} %multiply_convert_fusion.1), channel_id=1, source_target_pairs={{0,16},{4,20},{8,24},{12,28},{16,0},{20,4},{24,8},{28,12},{1,17},{... | collective-permute-start | bytes 786440 | tf_op jit(solution)/shard_map/ppermute | solution.py:17
  142.1 9.9 %collective-permute-done.16 = bf16[8,128,128]{2,1,0:T(8,128)(2,1)S(1)} collective-permute-done((bf16[8,128,128]{2,1,0:T(8,128)(2,1)S(1)}, bf16[8,128,128]{2,1,0:T(8,128)(2,1)S(1)}, u32[]{:S(2)}, u32[]{:S(2)}) %collective-permute-start.16) | collective-permute-done | bytes 262176 | tf_op jit(solution)/shard_map/ppermute | solution.py:17
  152.1 1.3 collective-permute-done.11
  155.0 9.8 %custom-call.6 = f32[1,128,128]{1,2,0:T(8,128)S(1)} custom-call(f32[1,128,128]{2,1,0:T(8,128)S(1)} %get-tuple-element.24), custom_call_target="InvertDiagBlocksLowerTriangular" | custom-call | tf_op jit(solution)/shard_map/triangular_solve | solution.py:265
  164.8 1.9 %convolution_multiply_fusion = f32[2048,128]{1,0:T(8,128)} fusion(f32[2048,128]{1,0:T(8,128)S(1)} %bitcast.43, f32[1,128,128]{1,2,0:T(8,128)S(1)} %custom-call.6), kind=kOutput, calls=%fused_computation.2 | convolution fusion | flops 402915328 | bytes 2162688 | tf_op jit(solution)/shard_map/triangular_solve | solution.py:265
  167.1 1.5 pad_maximum_fusion
  (61 shorter events, 13.3 us)
Async XLA Ops:
  21.8 2.9 %collective-permute-start = (bf16[2,16,128,128]{3,2,1,0:T(8,128)(2,1)}, bf16[2,16,128,128]{3,2,1,0:T(8,128)(2,1)S(1)}, u32[]{:S(2)}, u32[]{:S(2)}) collective-permute-start(bf16[2,16,128,128]{3,2,1,0:T(8,128)(2,1)} %get-tuple-element.10), channel_id=1, source_target_pairs={{0,1},{1,0},{2,3},{3,2},{4,5},{5,4},{6,7},{7,6},{8,9},{9,8},{10,11... | collective-permute-start | bytes 3145736 | tf_op jit(solution)/shard_map/ppermute | solution.py:17
  24.6 4.1 %copy-start.5 = (f32[8192]{0:T(1024)S(1)}, f32[8192]{0:T(1024)}, u32[]{:S(2)}) copy-start(f32[8192]{0:T(1024)} %param.11) | copy-start | bytes 98308
  24.6 28.6 %copy-start = (f32[2,16,128,128]{3,2,1,0:T(8,128)S(1)}, f32[2,16,128,128]{3,2,1,0:T(8,128)}, u32[]{:S(2)}) copy-start(f32[2,16,128,128]{3,2,1,0:T(8,128)} %get-tuple-element.9) | copy-start | bytes 6291460
  27.7 25.5 %collective-permute-start.1 = (bf16[2,16,128,128]{3,2,1,0:T(8,128)(2,1)}, bf16[2,16,128,128]{3,2,1,0:T(8,128)(2,1)}, u32[]{:S(2)}, u32[]{:S(2)}) collective-permute-start(bf16[2,16,128,128]{3,2,1,0:T(8,128)(2,1)} %fusion.1), channel_id=1, source_target_pairs={{0,2},{1,3},{2,0},{3,1},{4,6},{5,7},{6,4},{7,5},{8,10},{9,11},{10,... | collective-permute-start | bytes 3145736 | tf_op jit(solution)/shard_map/ppermute | solution.py:17
  28.8 28.1 %copy-start.4 = (s32[640]{0:T(1024)S(1)}, s32[640]{0:T(1024)}, u32[]{:S(2)}) copy-start(s32[640]{0:T(1024)} %reduce.7.dst) | copy-start | bytes 7684
  56.3 2.9 %collective-permute-start.7 = (bf16[32,128,128]{2,1,0:T(8,128)(2,1)}, bf16[32,128,128]{2,1,0:T(8,128)(2,1)S(1)}, u32[]{:S(2)}, u32[]{:S(2)}) collective-permute-start(bf16[32,128,128]{2,1,0:T(8,128)(2,1)} %bitcast.17.first), channel_id=1, source_target_pairs={{0,1},{1,0},{2,3},{3,2},{4,5},{5,4},{6,7},{7,6},{8,9},{9,8},{10,11... | collective-permute-start | bytes 3145736 | tf_op jit(solution)/shard_map/ppermute | solution.py:17
  59.1 1.0 copy-start.1
  74.4 31.1 %copy-start.2 = (f32[16,128,128]{2,1,0:T(8,128)S(1)}, f32[16,128,128]{2,1,0:T(8,128)}, u32[]{:S(2)}) copy-start(f32[16,128,128]{2,1,0:T(8,128)} %get-tuple-element.13) | copy-start | bytes 3145732
  74.4 30.2 %collective-permute-start.13 = (bf16[16,128,128]{2,1,0:T(8,128)(2,1)}, bf16[16,128,128]{2,1,0:T(8,128)(2,1)S(1)}, u32[]{:S(2)}, u32[]{:S(2)}) collective-permute-start(bf16[16,128,128]{2,1,0:T(8,128)(2,1)} %get-tuple-element.14), channel_id=1, source_target_pairs={{0,8},{4,12},{8,0},{12,4},{16,24},{20,28},{24,16},{28,20},{1,9},{5... | collective-permute-start | bytes 1572872 | tf_op jit(solution)/shard_map/ppermute | solution.py:17
  88.4 1.3 collective-permute-start.2
  89.8 4.3 %collective-permute-start.3 = (f32[128,128]{0,1:T(8,128)S(1)}, f32[128,128]{0,1:T(8,128)S(1)}, u32[]{:S(2)}, u32[]{:S(2)}) collective-permute-start(f32[128,128]{0,1:T(8,128)S(1)} %add.101), channel_id=1, source_target_pairs={{0,2},{1,3},{2,0},{3,1},{4,6},{5,7},{6,4},{7,5},{8,10},{9,11},{10,... | collective-permute-start | bytes 196616 | tf_op jit(solution)/shard_map/ppermute | solution.py:17
  94.1 6.1 %collective-permute-start.4 = (f32[128,128]{0,1:T(8,128)S(1)}, f32[128,128]{0,1:T(8,128)S(1)}, u32[]{:S(2)}, u32[]{:S(2)}) collective-permute-start(f32[128,128]{0,1:T(8,128)S(1)} %add.102), channel_id=1, source_target_pairs={{0,4},{4,0},{8,12},{12,8},{16,20},{20,16},{24,28},{28,24},{1,5},{5... | collective-permute-start | bytes 196616 | tf_op jit(solution)/shard_map/ppermute | solution.py:17
  97.6 13.6 %collective-permute-start.8 = (bf16[16,128,128]{2,1,0:T(8,128)(2,1)}, bf16[16,128,128]{2,1,0:T(8,128)(2,1)}, u32[]{:S(2)}, u32[]{:S(2)}) collective-permute-start(bf16[16,128,128]{2,1,0:T(8,128)(2,1)} %get-tuple-element.12), channel_id=1, source_target_pairs={{0,4},{4,0},{8,12},{12,8},{16,20},{20,16},{24,28},{28,24},{1,5},{5... | collective-permute-start | bytes 1572872 | tf_op jit(solution)/shard_map/ppermute | solution.py:17
  100.3 4.3 %collective-permute-start.5 = (f32[128,128]{0,1:T(8,128)S(1)}, f32[128,128]{0,1:T(8,128)S(1)}, u32[]{:S(2)}, u32[]{:S(2)}) collective-permute-start(f32[128,128]{0,1:T(8,128)S(1)} %add.103), channel_id=1, source_target_pairs={{0,8},{4,12},{8,0},{12,4},{16,24},{20,28},{24,16},{28,20},{1,9},{5... | collective-permute-start | bytes 196616 | tf_op jit(solution)/shard_map/ppermute | solution.py:17
  104.6 10.8 %collective-permute-start.6 = (f32[128,128]{0,1:T(8,128)S(1)}, f32[128,128]{0,1:T(8,128)S(1)}, u32[]{:S(2)}, u32[]{:S(2)}) collective-permute-start(f32[128,128]{0,1:T(8,128)S(1)} %add.104), channel_id=1, source_target_pairs={{0,16},{4,20},{8,24},{12,28},{16,0},{20,4},{24,8},{28,12},{1,17},{... | collective-permute-start | bytes 196616 | tf_op jit(solution)/shard_map/ppermute | solution.py:17
  104.7 0.8 copy-start.3
  107.4 14.1 %collective-permute-start.14 = (bf16[8,128,128]{2,1,0:T(8,128)(2,1)}, bf16[8,128,128]{2,1,0:T(8,128)(2,1)}, u32[]{:S(2)}, u32[]{:S(2)}) collective-permute-start(bf16[8,128,128]{2,1,0:T(8,128)(2,1)} %dynamic-slice_convert_fusion), channel_id=1, source_target_pairs={{0,16},{4,20},{8,24},{12,28},{16,0},{20,4},{24,8},{28,12},{1,17},{... | collective-permute-start | bytes 786440 | tf_op jit(solution)/shard_map/ppermute | solution.py:17
  113.4 11.7 %collective-permute-start.9 = (bf16[8,128,128]{2,1,0:T(8,128)(2,1)}, bf16[8,128,128]{2,1,0:T(8,128)(2,1)}, u32[]{:S(2)}, u32[]{:S(2)}) collective-permute-start(bf16[8,128,128]{2,1,0:T(8,128)(2,1)} %dynamic-slice_convert_fusion.1), channel_id=1, source_target_pairs={{0,8},{4,12},{8,0},{12,4},{16,24},{20,28},{24,16},{28,20},{1,9},{5... | collective-permute-start | bytes 786440 | tf_op jit(solution)/shard_map/ppermute | solution.py:17
  122.5 15.4 %collective-permute-start.15 = (bf16[8,128,128]{2,1,0:T(8,128)(2,1)S(1)}, bf16[8,128,128]{2,1,0:T(8,128)(2,1)S(1)}, u32[]{:S(2)}, u32[]{:S(2)}) collective-permute-start(bf16[8,128,128]{2,1,0:T(8,128)(2,1)S(1)} %add_convert_fusion), channel_id=1, source_target_pairs={{0,4},{4,0},{8,12},{12,8},{16,20},{20,16},{24,28},{28,24},{1,5},{5... | collective-permute-start | bytes 786440 | tf_op jit(solution)/shard_map/ppermute | solution.py:17
  126.1 15.0 %collective-permute-start.10 = (bf16[8,128,128]{2,1,0:T(8,128)(2,1)S(1)}, bf16[8,128,128]{2,1,0:T(8,128)(2,1)S(1)}, u32[]{:S(2)}, u32[]{:S(2)}) collective-permute-start(bf16[8,128,128]{2,1,0:T(8,128)(2,1)S(1)} %add_convert_fusion.1), channel_id=1, source_target_pairs={{0,16},{4,20},{8,24},{12,28},{16,0},{20,4},{24,8},{28,12},{1,17},{... | collective-permute-start | bytes 786440 | tf_op jit(solution)/shard_map/ppermute | solution.py:17
  138.1 13.8 %collective-permute-start.16 = (bf16[8,128,128]{2,1,0:T(8,128)(2,1)S(1)}, bf16[8,128,128]{2,1,0:T(8,128)(2,1)S(1)}, u32[]{:S(2)}, u32[]{:S(2)}) collective-permute-start(bf16[8,128,128]{2,1,0:T(8,128)(2,1)S(1)} %multiply_convert_fusion.1), channel_id=1, source_target_pairs={{0,16},{4,20},{8,24},{12,28},{16,0},{20,4},{24,8},{28,12},{1,17},{... | collective-permute-start | bytes 786440 | tf_op jit(solution)/shard_map/ppermute | solution.py:17
  141.3 12.1 %collective-permute-start.11 = (bf16[8,128,128]{2,1,0:T(8,128)(2,1)S(1)}, bf16[8,128,128]{2,1,0:T(8,128)(2,1)S(1)}, u32[]{:S(2)}, u32[]{:S(2)}) collective-permute-start(bf16[8,128,128]{2,1,0:T(8,128)(2,1)S(1)} %multiply_convert_fusion.2), channel_id=1, source_target_pairs={{0,8},{4,12},{8,0},{12,4},{16,24},{20,28},{24,16},{28,20},{1,9},{5... | collective-permute-start | bytes 786440 | tf_op jit(solution)/shard_map/ppermute | solution.py:17
  152.0 14.7 %collective-permute-start.17 = (bf16[16,128,128]{2,1,0:T(8,128)(2,1)S(1)}, bf16[16,128,128]{2,1,0:T(8,128)(2,1)S(1)}, u32[]{:S(2)}, u32[]{:S(2)}) collective-permute-start(bf16[16,128,128]{2,1,0:T(8,128)(2,1)S(1)} %maximum_select_fusion.3), channel_id=1, source_target_pairs={{0,8},{4,12},{8,0},{12,4},{16,24},{20,28},{24,16},{28,20},{1,9},{5... | collective-permute-start | bytes 1572872 | tf_op jit(solution)/shard_map/ppermute | solution.py:17
  153.5 13.4 %collective-permute-start.12 = (bf16[16,128,128]{2,1,0:T(8,128)(2,1)S(1)}, bf16[16,128,128]{2,1,0:T(8,128)(2,1)S(1)}, u32[]{:S(2)}, u32[]{:S(2)}) collective-permute-start(bf16[16,128,128]{2,1,0:T(8,128)(2,1)S(1)} %maximum_select_fusion.2), channel_id=1, source_target_pairs={{0,4},{4,0},{8,12},{12,8},{16,20},{20,16},{24,28},{28,24},{1,5},{5... | collective-permute-start | bytes 1572872 | tf_op jit(solution)/shard_map/ppermute | solution.py:17

commit v2 on v0

v2 whole, which is shorter than its diff:
```python
import functools
import math

import jax
import jax.numpy as jnp
from jax import lax
from jax.experimental import pallas as pl
from jax.experimental.pallas import tpu as pltpu
from jax.experimental.layout import Layout, with_layout_constraint
from jax.sharding import PartitionSpec as P

F32 = jnp.float32
BF16 = jnp.bfloat16


def row_major(x):
    return with_layout_constraint(x, Layout(major_to_minor=tuple(range(x.ndim))))


def swap(x, axis, bit):
    n = lax.axis_size(axis)
    return row_major(lax.ppermute(row_major(x), axis, [(i, i ^ (1 << bit)) for i in range(n)]))


def bit_of(axis, bit):
    return (lax.axis_index(axis) >> bit) & 1


UNROLL = 32


def iota(shape, dim):
    return lax.broadcasted_iota(jnp.int32, shape, dim)


def ones_where(mask, dtype=BF16):
    return jnp.where(mask, 1.0, 0.0).astype(dtype)


def build_list(groups, places, key, live, values):
    slots = key.shape[1]
    member = jnp.where((key == iota((groups, slots), 0)) & live, 1.0, 0.0)
    earlier = ones_where(iota((slots, slots), 0) < iota((slots, slots), 1))
    within = jnp.dot(member.astype(BF16), earlier, preferred_element_type=F32)
    size = 2.0 * jnp.floor((jnp.sum(member, axis=1, keepdims=True) + 1.0) * 0.5)
    lower = ones_where(iota((groups, groups), 1) < iota((groups, groups), 0))
    spread = jnp.broadcast_to(size, (groups, 128)).astype(BF16)
    first = jnp.dot(lower, spread, preferred_element_type=F32)[:, :1]
    place = jnp.sum(member * (within + first), axis=0, keepdims=True)
    place = jnp.where(live, place, -1.0).astype(jnp.int32)
    taken = ones_where(place == iota((places, slots), 0))
    row = iota((8, slots), 0)
    stacked = jnp.where(row == 0, 1, 0)
    for i, value in enumerate(values):
        stacked = jnp.where(row == i + 1, value, stacked)
    found = lax.dot_general(
        stacked.astype(F32).astype(BF16), taken, (((1,), (1,)), ((), ())), preferred_element_type=F32
    )
    return [found[i + 1 : i + 2] for i in range(len(values))], found[0:1], size


def pack_rows(rows, places):
    row = iota((8, places), 0)
    packed = jnp.zeros((8, places), F32)
    for i, value in enumerate(rows):
        packed = jnp.where(row == i, value, packed)
    return packed.astype(jnp.int32)


def add_pair(transposed, tiles, at, panel, places, acc, to):
    two = [tiles[at[0]], tiles[at[1]]]
    panels = jnp.concatenate([panel[places[0]], panel[places[1]]], axis=0)
    if transposed:
        dims = (((0,), (0,)), ((), ()))
        left = jnp.concatenate(two, axis=0)
    else:
        dims = (((1,), (0,)), ((), ()))
        left = jnp.concatenate(two, axis=1)
    acc[to] += lax.dot_general(left, panels, dims, preferred_element_type=F32)


def split_out(acc, base, shares, size, core, own, send):
    for h in range(shares // 2):

        def block(i, carry):
            own[h * size + i] = acc[base + (2 * h + core) * size + i]
            send[h * size + i] = acc[base + (2 * h + 1 - core) * size + i].astype(BF16)
            return carry

        lax.fori_loop(0, size, block, 0, unroll=2)


def fetch(order, first, tiles, held, sem, chunk):
    slots = sem.shape[0]
    slot = lax.rem(chunk, slots)
    for j in range(2 * UNROLL):
        tile = order[0, first + chunk * 2 * UNROLL + j]
        pltpu.make_async_copy(tiles.at[tile], held.at[slot * 2 * UNROLL + j], sem.at[slot]).start()


def multiply(transposed, order, first, pairs, dead, tiles, held, sem, panel, acc, ahead=lambda: None):
    slots = sem.shape[0]
    chunks = pl.cdiv(pairs, UNROLL)

    def begin(chunk, carry):
        fetch(order, first, tiles, held, sem, chunk)
        return carry

    lax.fori_loop(0, jnp.minimum(chunks, slots), begin, 0)
    ahead()

    def work(chunk, carry):
        slot = lax.rem(chunk, slots)
        whole = pl.ds(slot * 2 * UNROLL, 2 * UNROLL)
        pltpu.make_async_copy(tiles.at[pl.ds(0, 2 * UNROLL)], held.at[whole], sem.at[slot]).wait()
        for j in range(UNROLL):
            q = chunk * UNROLL + j
            p = first + 2 * q
            h = slot * 2 * UNROLL + 2 * j
            to = jnp.where(q < pairs, order[2, p], dead)
            add_pair(transposed, held, (h, h + 1), panel, (order[1, p], order[1, p + 1]), acc, to)

        @pl.when(chunk + slots < chunks)
        def _():
            fetch(order, first, tiles, held, sem, chunk + slots)

        return carry

    lax.fori_loop(0, chunks, work, 0)


def shares_of(row, share):
    return row >> (share.bit_length() - 1), row & (share - 1)


def order_rows(found, taken, size, blocks, groups):
    high, low, source, target = found
    return [
        high * 64.0 + low,
        source + (1.0 - taken) * blocks,
        target + (1.0 - taken) * groups,
        0.5 * jnp.sum(size, axis=0, keepdims=True),
    ]


def image_kernel(
    shares, cut, meta, rows_h, cols_h, degree_h, start, tiles,
    own_one, own_two, send,
    acc, rows, cols, degree, panel, order, order_s, held, in_sem, order_sem, tile_sem,
):
    groups = degree.shape[0]
    share = groups // shares
    slots = rows.shape[1]
    places = order.shape[1]
    copies = [
        pltpu.make_async_copy(source, target, in_sem.at[i])
        for i, (source, target) in enumerate(
            ((rows_h, rows), (cols_h, cols), (degree_h, degree), (start, panel.at[pl.ds(0, groups)]))
        )
    ]
    for copy in copies:
        copy.start()
    count, core = meta[0], meta[1]
    copies[0].wait()
    copies[1].wait()
    lane = iota((1, slots), 1)
    row, col = rows[...], cols[...]
    part, at = shares_of(row, share)
    key = jnp.where(at < cut, part * cut + at, shares * cut + part * (share - cut) + at - cut)
    found, taken, size = build_list(
        groups, places, key, lane < count, [lane >> 6, lane & 63, col, key]
    )
    order[...] = pack_rows(order_rows(found, taken, size, groups, groups), places)
    order_copy = pltpu.make_async_copy(order, order_s, order_sem)
    order_copy.start()
    acc[...] = jnp.zeros_like(acc)
    order_copy.wait()

    def ahead():
        copies[2].wait()
        copies[3].wait()
        scale = lax.transpose(lax.rsqrt(degree[...]), (1, 0))
        for g in range(groups):
            panel[g] = (panel[g].astype(F32) * scale[:, g : g + 1]).astype(BF16)
        panel[groups] = jnp.zeros(panel.shape[1:], BF16)

    multiply(False, order_s, 0, order_s[3, 0], groups, tiles, held, tile_sem, panel, acc, ahead)
    split_out(acc, 0, shares, cut, core, own_one, send.at[pl.ds(0, own_one.shape[0])])
    split_out(
        acc, shares * cut, shares, share - cut, core, own_two,
        send.at[pl.ds(own_one.shape[0], own_two.shape[0])],
    )


def order_kernel(shares, cut, groups, meta, rows, cols, back_one, back_two):
    share = groups // shares
    slots = rows.shape[1]
    places = back_one.shape[1]
    count, core = meta[0], meta[1]
    lane = iota((1, slots), 1)
    row, col = rows[...], cols[...]
    part, at = shares_of(row, share)
    for out, size, piece, inside in (
        (back_one, cut, at < cut, at),
        (back_two, share - cut, at >= cut, at - cut),
    ):
        blocks = shares * size
        place = ((part & 1) ^ core) * (blocks // 2) + (part >> 1) * size + inside
        found, taken, padded = build_list(
            groups, places, col, (lane < count) & piece, [lane >> 6, lane & 63, place, col]
        )
        out[...] = pack_rows(order_rows(found, taken, padded, blocks, groups), places)


def caption_part(order, tiles, mine, other, acc, panel, held, sem, tile_sem, fill):
    half = mine.shape[0]
    copies = [
        pltpu.make_async_copy(source, panel.at[pl.ds(i * half, half)], sem.at[i])
        for i, source in enumerate((mine, other))
    ]

    def ahead():
        for copy in copies:
            copy.start()
        panel[2 * half] = jnp.zeros(panel.shape[1:], BF16)
        fill()
        for copy in copies:
            copy.wait()

    multiply(
        True, order, 0, order[3, 0], acc.shape[0] - 1, tiles, held, tile_sem, panel, acc, ahead
    )


def third_kernel(order, tiles, mine, other, acc, mark, panel, held, sem, tile_sem):
    mark[...] = jnp.zeros_like(mark)

    def fill():
        acc[...] = jnp.zeros_like(acc)

    caption_part(order, tiles, mine, other, acc, panel, held, sem, tile_sem, fill)


def fourth_kernel(
    meta, order, tiles, before_h, mine, other, own_a, send_a, own_b, send_b,
    acc, before, panel, held, sem, before_sem, tile_sem,
):
    copy = pltpu.make_async_copy(before_h, before, before_sem)
    copy.start()

    def fill():
        acc[...] = jnp.zeros_like(acc)

    caption_part(order, tiles, mine, other, acc, panel, held, sem, tile_sem, fill)
    copy.wait()
    part = own_a.shape[0]
    for own, send, base, bit in ((own_a, send_a, 0, meta[0]), (own_b, send_b, 2 * part, meta[1])):

        def block(i, carry):
            keep, give = base + bit * part + i, base + (1 - bit) * part + i
            own[i] = acc[keep] + before[keep]
            send[i] = (acc[give] + before[give]).astype(BF16)
            return carry

        lax.fori_loop(0, part, block, 0, unroll=2)


def factor_kernel(root, gram, upper, inverse, rest, left):
    size = gram.shape[0]
    rest[...] = gram[...]
    left[...] = ones_where(iota((size, size), 0) == iota((size, size), 1), F32)
    row = iota((8, size), 0)
    for base in range(0, size, 8):
        panel = pl.ds(base, 8)
        u, m = rest[panel, :], left[panel, :]
        columns = [jnp.broadcast_to(u[:, base + k : base + k + 1], (8, size)) for k in range(8)]
        scale = jnp.zeros((8, size), F32)
        for s in range(8):
            pivot = columns[s][s : s + 1]
            scale = jnp.where(row == s, lax.rsqrt(pivot), scale)
            f = jnp.where(row > s, columns[s] / pivot, 0.0)
            for k in range(s + 1, 8):
                columns[k] = columns[k] - f * columns[k][s : s + 1]
            u = u - f * u[s : s + 1]
            m = m - f * m[s : s + 1]
        u = jnp.where(iota((8, size), 1) >= row + base, u * scale, 0.0)
        m = m * scale
        upper[panel, :] = u * (1.0 / root)
        inverse[panel, :] = m * root
        if base + 8 < size:
            both = lax.dot_general(
                u,
                jnp.concatenate([u, m], axis=1),
                (((0,), (0,)), ((), ())),
                precision=lax.Precision.HIGHEST,
                preferred_element_type=F32,
            )
            rest[...] -= both[:, :size]
            left[...] -= both[:, size:]


VMEM = pl.BlockSpec(memory_space=pltpu.VMEM)
SMEM = pl.BlockSpec(memory_space=pltpu.SMEM)
ANY = pl.BlockSpec(memory_space=pl.ANY)
HBM = pl.BlockSpec(memory_space=pltpu.HBM)
PARAMS = pltpu.CompilerParams(vmem_limit_bytes=32 * 2**20)
DEPTH = 4


def in_hbm(x):
    return pltpu.with_memory_space_constraint(x, pltpu.HBM)


def buffers(tile):
    return [
        pltpu.VMEM((DEPTH * 2 * UNROLL, tile, tile), BF16),
        pltpu.SemaphoreType.DMA((DEPTH,)),
    ]


def places_of(slots, groups):
    return (pl.cdiv(slots + groups, 2 * UNROLL) + 1) * 2 * UNROLL


def forward(shares, cut, meta, rows, cols, degree, start, tiles):
    slots, tile, _ = tiles.shape
    groups, _, width = start.shape
    places = places_of(slots, groups)
    block = (tile, width)
    one = shares // 2 * cut
    two = groups // 2 - one
    held, tile_sem = buffers(tile)
    return pl.pallas_call(
        functools.partial(image_kernel, shares, cut),
        in_specs=[SMEM] + [HBM] * 5,
        out_specs=[VMEM] * 3,
        out_shape=[
            jax.ShapeDtypeStruct((one, *block), F32),
            jax.ShapeDtypeStruct((two, *block), F32),
            jax.ShapeDtypeStruct((one + two, *block), BF16),
        ],
        scratch_shapes=[
            pltpu.VMEM((groups + 1, *block), F32),
            pltpu.VMEM((1, slots), jnp.int32),
            pltpu.VMEM((1, slots), jnp.int32),
            pltpu.VMEM((groups, tile), F32),
            pltpu.VMEM((groups + 1, *block), BF16),
            pltpu.VMEM((8, places), jnp.int32),
            pltpu.SMEM((8, places), jnp.int32),
            held,
            pltpu.SemaphoreType.DMA((4,)),
            pltpu.SemaphoreType.DMA,
            tile_sem,
        ],
        compiler_params=PARAMS,
        name="image",
    )(meta, *map(in_hbm, (rows, cols, degree, start, tiles)))


def back_orders(shares, cut, groups, meta, rows, cols):
    listing = jax.ShapeDtypeStruct((8, places_of(rows.shape[1], groups)), jnp.int32)
    return pl.pallas_call(
        functools.partial(order_kernel, shares, cut, groups),
        in_specs=[SMEM, VMEM, VMEM],
        out_specs=[VMEM] * 2,
        out_shape=[listing] * 2,
        compiler_params=PARAMS,
        name="orders",
    )(meta, rows, cols)


def backward_one(groups, order, tiles, mine, other):
    block = mine.shape[1:]
    held, tile_sem = buffers(block[0])
    return pl.pallas_call(
        third_kernel,
        in_specs=[SMEM, HBM, ANY, ANY],
        out_specs=[VMEM] * 2,
        out_shape=[
            jax.ShapeDtypeStruct((groups + 1, *block), F32),
            jax.ShapeDtypeStruct((1, 128), F32),
        ],
        scratch_shapes=[
            pltpu.VMEM((2 * mine.shape[0] + 1, *block), BF16),
            held,
            pltpu.SemaphoreType.DMA((2,)),
            tile_sem,
        ],
        compiler_params=PARAMS,
        name="caption_one",
    )(order, in_hbm(tiles), mine, other)


def backward_two(groups, meta, order, tiles, before, mine, other):
    block = mine.shape[1:]
    part = groups // 4
    held, tile_sem = buffers(block[0])
    total = pltpu.VMEM((groups + 1, *block), F32)
    return pl.pallas_call(
        fourth_kernel,
        in_specs=[SMEM, SMEM, HBM, HBM, ANY, ANY],
        out_specs=[VMEM] * 4,
        out_shape=[
            jax.ShapeDtypeStruct((part, *block), F32),
            jax.ShapeDtypeStruct((part, *block), BF16),
        ]
        * 2,
        scratch_shapes=[
            total,
            total,
            pltpu.VMEM((2 * mine.shape[0] + 1, *block), BF16),
            held,
            pltpu.SemaphoreType.DMA((2,)),
            pltpu.SemaphoreType.DMA,
            tile_sem,
        ],
        compiler_params=PARAMS,
        name="caption_two",
    )(meta, order, in_hbm(tiles), in_hbm(before), mine, other)


def factorize(gram, root):
    shape = jax.ShapeDtypeStruct(gram.shape, F32)
    return pl.pallas_call(
        functools.partial(factor_kernel, root),
        in_specs=[VMEM],
        out_specs=[VMEM] * 2,
        out_shape=[shape] * 2,
        scratch_shapes=[pltpu.VMEM(gram.shape, F32)] * 2,
        name="factorize",
    )(gram)


def halves(x, bit):
    n = x.shape[0] // 2
    return (
        lax.dynamic_slice_in_dim(x, bit * n, n, 0),
        lax.dynamic_slice_in_dim(x, (1 - bit) * n, n, 0),
    )


def joined(own, other, bit):
    return jnp.where(bit == 0, jnp.concatenate([own, other]), jnp.concatenate([other, own]))


def rounded(x):
    return lax.reduce_precision(x, exponent_bits=8, mantissa_bits=7).astype(BF16)


def in_two(x):
    high = rounded(x)
    return jnp.stack([high, rounded(x - high.astype(F32))])


def from_two(x):
    return x[0].astype(F32) + x[1].astype(F32)


def swap_with(x, extra, axis, bit):
    size = x.shape[0]
    arrived = swap(jnp.concatenate([x, extra]), axis, bit)
    return arrived[:size], in_two(from_two(extra) + from_two(arrived[size:]))


def reduce_rest(own, arrived, bits, extra=None):
    parts = [own, arrived]
    for i, bit in enumerate(bits[1:]):
        last = i == len(bits) - 2
        if last:
            give = rounded(sum(x.astype(F32) for x in parts))
            parts = [give]
        else:
            split = [halves(x, bit_of("img", bit)) for x in parts]
            give = rounded(sum(x.astype(F32) for _, x in split))
            parts = [x for x, _ in split]
        if extra is None:
            arrived = swap(give, "img", bit)
        else:
            arrived, extra = swap_with(give, extra, "img", bit)
        parts.append(arrived)
    return sum(x.astype(F32) for x in parts), extra


def scatter_start(x, bits):
    for bit in bits[:-1]:
        x = halves(x, bit_of("img", bit))[0]
    return x


def gather_back(x, bits, extra=None, along=None):
    for bit in reversed(bits[:-1]):
        if bit == along:
            arrived, extra = swap_with(x, extra, "img", bit)
        else:
            arrived = swap(x, "img", bit)
        x = joined(x, arrived, bit_of("img", bit))
    return x, extra


def body(tile_values, tile_rows, tile_cols, tile_count, row_degree, col_degree, start_panel):
    slots, tile, _ = tile_values.shape
    width = start_panel.shape[1]
    row_total = row_degree.shape[0]
    col_total = col_degree.shape[0]
    row_groups = row_total // tile
    col_groups = col_total // tile
    caps = lax.axis_size("cap")
    imgs = lax.axis_size("img")
    cap_bits = caps.bit_length() - 1
    img_bits = imgs.bit_length() - 1
    core = bit_of("cap", 0)
    chip = lax.axis_index("cap") >> 1
    root = math.sqrt(row_total * imgs)
    share = row_groups // caps
    cut = share // 2
    count = tile_count[0, 0]
    row_scale = (1.0 / jnp.sqrt(row_degree)).reshape(caps // 2, 2, share, tile, 1)
    row_scale = lax.dynamic_index_in_dim(row_scale, core, 1, False)
    col_scale = (1.0 / jnp.sqrt(col_degree)).reshape(col_groups, tile, 1)
    degree = col_degree.reshape(col_groups, tile)
    start = start_panel.reshape(col_groups, tile, width)

    meta = jnp.stack([count, core])
    own_one, own_two, send = forward(
        caps, cut, meta, tile_rows, tile_cols, degree, start, tile_values
    )
    came = swap(send, "cap", 0)
    size = own_one.shape[0]
    first = rounded(own_one + came[:size].astype(F32))
    second = rounded(own_two + came[size:].astype(F32))
    order_one, order_two = back_orders(caps, cut, col_groups, meta, tile_rows, tile_cols)

    def over_chips(part):
        part = part.astype(F32)
        for bit in range(1, cap_bits):
            part = rounded(part)
            part = part.astype(F32) + swap(part, "cap", bit).astype(F32)
        return part

    def finish(part, scale):
        scale = scale.reshape(-1, tile, 1)
        image = part * scale
        mine = (image * scale).astype(BF16)
        return image, mine, swap(mine, "cap", 0)

    def products(image):
        flat = image.reshape(-1, width)
        return jnp.dot(flat.T, flat, precision=lax.Precision.HIGHEST, preferred_element_type=F32)

    scale_one, scale_two = row_scale[:, :cut], row_scale[:, cut:]
    order_one, scale_one = lax.optimization_barrier((order_one, scale_one))
    first, second = over_chips(first), over_chips(second)
    image_one, mine, other = finish(first, scale_one)
    gram = products(image_one)
    before, mark = backward_one(col_groups, order_one, tile_values, mine, other)
    gram, scale_two = lax.optimization_barrier((gram, scale_two + mark[0, 0]))
    image_two, mine, other = finish(second, scale_two)

    order_a = list(range(img_bits))
    order_b = [1, 0, *range(2, img_bits)]
    own_a, send_a, own_b, send_b = backward_two(
        col_groups,
        jnp.stack([bit_of("img", order_a[0]), bit_of("img", order_b[0])]),
        order_two,
        tile_values,
        before,
        mine,
        other,
    )
    send_a, send_b, image_two = lax.optimization_barrier((send_a, send_b, image_two))
    scale_a, scale_b = col_scale[: col_groups // 2], col_scale[col_groups // 2 :]
    got_a = swap(send_a, "img", order_a[0])
    got_b = swap(send_b, "img", order_b[0])
    gram = gram + products(image_two)
    gram = in_two(gram + swap(gram, "cap", 0))
    sum_a, gram = reduce_rest(own_a, got_a, order_a, gram)
    sum_b, _ = reduce_rest(own_b, got_b, order_b)
    next_a = (sum_a * scatter_start(scale_a, order_a)).astype(BF16)
    next_b = (sum_b * scatter_start(scale_b, order_b)).astype(BF16)
    next_b, gram = gather_back(next_b, order_b, gram, order_a[0])
    next_a, _ = gather_back(next_a, order_a)
    next_panel = jnp.concatenate([next_a, next_b]).reshape(col_total, width)

    factor, inverse = factorize(from_two(gram), root)
    rows = jnp.concatenate(
        [
            lax.dynamic_index_in_dim(image.reshape(caps // 2, -1, tile, width), chip, 0, False)
            for image in (image_one, image_two)
        ]
    ).reshape(share * tile, width)
    basis = lax.dot_general(
        rows,
        inverse,
        (((1,), (1,)), ((), ())),
        precision=lax.Precision.HIGHEST,
        preferred_element_type=F32,
    )
    return (basis, factor, next_panel)


def solution(mesh):
    placed = (
        P("img", "cap", None),
        P("img", "cap"),
        P("img", "cap"),
        P("img", "cap"),
        P("img"),
        P("cap"),
        P("cap", None),
    )
    return jax.shard_map(
        body,
        mesh=mesh,
        in_specs=placed,
        out_specs=(P(("img", "cap"), None), P(), P("cap", None)),
        check_vma=False,
    )
```

time: 522 us -> 145 us (0.28)
  local copies, waits for them, and re-layouts: 133 us -> 2.13 us
  matrix products: 130 us -> 6.53 us
  waiting for transfers between devices: 168 us -> 65 us
  blocking collectives: 39.4 us -> 0 us
  Pallas kernels: 0 us -> 37.9 us
  other arithmetic: 34.1 us -> 5 us
  starting transfers between devices: 0.26 us -> 28 us
  between operations: 14.8 us -> 1.62 us
    psum x2 -> x0, waiting for transfers between devices: 168 us -> none  [the longest x1 87.6 us: body(): image_panel = lax.psum(image_terms, 'cap') * row_scale[:, None]]
    dot_general x5 -> x3, matrix products: 127 us -> 6.53 us  [the longest x2 3.73 us: products(): jnp.dot(flat.T, flat, precision=lax.Precision.HIGHEST, preferred_element_...]
    dot_general x2 -> x0, local copies, waits for them, and re-layouts: 88.1 us -> none  [the longest x1 44.1 us: body(): jnp.einsum('tbc,tck->tbk', tile_values, gathered, preferred_element_type=...]
    ppermute x0 -> x16, waiting for transfers between devices: none -> 65 us  [swap(): lax.ppermute(row_major(x), axis, [(i, i ^ 1 << bit) for i in range(n)])]
    psum x1 -> x0, blocking collectives: 39.4 us -> none  [body(): lax.psum(jnp.dot(image_panel.T, image_panel, precision=lax.Precision.HIGH...]
    pallas_call x0 -> x5, Pallas kernels: none -> 37.9 us  [the longest x1 12.5 us: forward(): pl.pallas_call(functools.partial(image_kernel, shares, cut), in_specs=[SM...]
    gather x2 -> x0, local copies, waits for them, and re-layouts: 33.1 us -> none  [the longest x1 16.6 us: body(): picked = scaled_image.reshape(row_groups, tile_size, width)[rows]]
    ppermute x0 -> x16, starting transfers between devices: none -> 28 us  [swap(): lax.ppermute(row_major(x), axis, [(i, i ^ 1 << bit) for i in range(n)])]
  transfers between devices with their start and end apart: 2 -> 16, of which waited for: 2 -> 11; matrix products, arithmetic and copies ran while one was open for 7% -> 6% of each run, Pallas kernels for 0% -> 12%
where the time goes in v2:
time: 145 us; the launch traced here: 146 us
  waiting for transfers between devices  65 us (45%)
  Pallas kernels  37.9 us (26%)
  starting transfers between devices  28 us (19%)
  matrix products  6.53 us (5%)
  other arithmetic  5 us (3%)
  local copies, waits for them, and re-layouts  2.13 us (1%)
  between operations  1.62 us (1%)
    ppermute x16, waiting for transfers between devices, swap(): lax.ppermute(row_major(x), axis, [(i, i ^ 1 << bit) for i in range(n)])  65 us
    ppermute x16, starting transfers between devices, swap(): lax.ppermute(row_major(x), axis, [(i, i ^ 1 << bit) for i in range(n)])  28 us
    pallas_call x1, Pallas kernels, forward(): pl.pallas_call(functools.partial(image_kernel, shares, cut), in_specs=[SM...  12.5 us
    pallas_call x1, Pallas kernels, factorize(): pl.pallas_call(functools.partial(factor_kernel, root), in_specs=[VMEM], o...  9.96 us
    pallas_call x1, Pallas kernels, backward_two(): pl.pallas_call(fourth_kernel, in_specs=[SMEM, SMEM, HBM, HBM, ANY, ANY],...  7.96 us
    pallas_call x1, Pallas kernels, backward_one(): pl.pallas_call(third_kernel, in_specs=[SMEM, HBM, ANY, ANY], out_specs=[V...  5.68 us
    dot_general x2, matrix products, products(): jnp.dot(flat.T, flat, precision=lax.Precision.HIGHEST, preferred_element_...  3.73 us
  transfers between devices with their start and end apart: 16, of which 11 were waited for; matrix products, arithmetic and copies ran while one was open for 6% of the time, Pallas kernels for 12%

profile of v2, /device:TPU:0, one launch (start us, length us, event | category | flops | bytes accessed | tf_op | source)
XLA Modules:
  0.0 146.2 jit_solution(7097161604432250313)
XLA Ops:
  1.4 12.5 %image.1 = (f32[16,128,128]{2,1,0:T(8,128)S(1)}, f32[16,128,128]{2,1,0:T(8,128)S(1)}, bf16[32,128,128]{2,1,0:T(8,128)(2,1)S(1)}) custom-call(s32[2]{0:T(128)S(1)} %pad_add_fusion.meta, s32[1,640]{1,0:T(1,128)} %rows.1, s32[1,640]{1,0:T(1,128)} %cols.1, f32[64,128]{1,0:T(8,128)} %bitcast.75, bf16[64,128,128]{2,1,0:T(8,128)(2,1)} %bitcast.74, ...), custom_call_target="tpu_custom_call" | custom-call | tf_op jit(solution)/shard_map/image/pallas_call | solution.py:333
  13.9 2.6 %collective-permute-done = bf16[32,128,128]{2,1,0:T(8,128)(2,1)S(1)} collective-permute-done((bf16[32,128,128]{2,1,0:T(8,128)(2,1)S(1)}, bf16[32,128,128]{2,1,0:T(8,128)(2,1)S(1)}, u32[]{:S(2)}, u32[]{:S(2)}) %collective-permute-start) | collective-permute-done | bytes 1048608 | tf_op jit(solution)/shard_map/ppermute | solution.py:22
  16.9 3.5 %collective-permute-start.1 = (bf16[16,128,128]{2,1,0:T(8,128)(2,1)S(1)}, bf16[16,128,128]{2,1,0:T(8,128)(2,1)S(1)}, u32[]{:S(2)}, u32[]{:S(2)}) collective-permute-start(bf16[16,128,128]{2,1,0:T(8,128)(2,1)S(1)} %get-tuple-element.50), channel_id=1, source_target_pairs={{0,2},{1,3},{2,0},{3,1},{4,6},{5,7},{6,4},{7,5},{8,10},{9,11},{10,... | collective-permute-start | bytes 1572872 | tf_op jit(solution)/shard_map/ppermute | solution.py:22
  20.3 1.8 %orders.1 = (s32[8,768]{1,0:T(8,128)S(1)}, s32[8,768]{1,0:T(8,128)S(1)}) custom-call(s32[2]{0:T(128)S(1)} %pad_add_fusion.meta, s32[1,640]{1,0:T(1,128)S(1)} %copy-done.1, s32[1,640]{1,0:T(1,128)S(1)} %copy-done.2), custom_call_target="tpu_custom_call" | custom-call | tf_op jit(solution)/shard_map/orders/pallas_call | solution.py:362
  22.2 10.3 %collective-permute-done.1 = bf16[16,128,128]{2,1,0:T(8,128)(2,1)S(1)} collective-permute-done((bf16[16,128,128]{2,1,0:T(8,128)(2,1)S(1)}, bf16[16,128,128]{2,1,0:T(8,128)(2,1)S(1)}, u32[]{:S(2)}, u32[]{:S(2)}) %collective-permute-start.1) | collective-permute-done | bytes 524320 | tf_op jit(solution)/shard_map/ppermute | solution.py:22
  33.0 1.8 %collective-permute-start.3 = (bf16[16,128,128]{2,1,0:T(8,128)(2,1)S(1)}, bf16[16,128,128]{2,1,0:T(8,128)(2,1)S(1)}, u32[]{:S(2)}, u32[]{:S(2)}) collective-permute-start(bf16[16,128,128]{2,1,0:T(8,128)(2,1)S(1)} %get-tuple-element.49), channel_id=1, source_target_pairs={{0,2},{1,3},{2,0},{3,1},{4,6},{5,7},{6,4},{7,5},{8,10},{9,11},{10,... | collective-permute-start | bytes 1572872 | tf_op jit(solution)/shard_map/ppermute | solution.py:22
  34.8 1.9 %convolution_bitcast_fusion.1 = f32[128,128]{1,0:T(8,128)S(1)} fusion(f32[16,128,128]{2,1,0:T(8,128)S(1)} %get-tuple-element.46), kind=kOutput, calls=%fused_computation.2 | convolution fusion | flops 402653184 | bytes 1114112 | tf_op jit(solution)/shard_map/dot_general | solution.py:548
  36.7 5.7 %caption_one.1 = (f32[65,128,128]{2,1,0:T(8,128)S(1)}, f32[1,128]{1,0:T(1,128)S(1)}) custom-call(s32[8,768]{1,0:T(8,128)S(1)} %get-tuple-element.28.order, bf16[640,128,128]{2,1,0:T(8,128)(2,1)} %tiles.5, bf16[16,128,128]{2,1,0:T(8,128)(2,1)S(1)} %get-tuple-element.45.mine, bf16[16,128,128]{2,1,0:T(8,128)(2,1)S(1)} %collective-permute-done.2.other), custom_call_target="tpu_custom_call" | custom-call | tf_op jit(solution)/shard_map/caption_one/pallas_call | solution.py:375
  42.4 2.0 %copy-done = f32[65,128,128]{2,1,0:T(8,128)} copy-done((f32[65,128,128]{2,1,0:T(8,128)}, f32[65,128,128]{2,1,0:T(8,128)S(1)}, u32[]{:S(2)}) %copy-start) | copy-done | bytes 4259864
  44.4 2.9 %collective-permute-done.3 = bf16[16,128,128]{2,1,0:T(8,128)(2,1)S(1)} collective-permute-done((bf16[16,128,128]{2,1,0:T(8,128)(2,1)S(1)}, bf16[16,128,128]{2,1,0:T(8,128)(2,1)S(1)}, u32[]{:S(2)}, u32[]{:S(2)}) %collective-permute-start.3) | collective-permute-done | bytes 524320 | tf_op jit(solution)/shard_map/ppermute | solution.py:22
  47.7 1.0 collective-permute-start.4
  48.9 1.4 collective-permute-done.4.other
  50.3 8.0 %caption_two.1 = (f32[16,128,128]{2,1,0:T(8,128)S(1)}, bf16[16,128,128]{2,1,0:T(8,128)(2,1)S(1)}, f32[16,128,128]{2,1,0:T(8,128)S(1)}, bf16[16,128,128]{2,1,0:T(8,128)(2,1)S(1)}) custom-call(s32[2]{0:T(128)S(1)} %pad_add_fusion.1.meta, s32[8,768]{1,0:T(8,128)S(1)} %get-tuple-element.27.order, bf16[640,128,128]{2,1,0:T(8,128)(2,1)} %tiles.5, ...), custom_call_target="tpu_custom_call" | custom-call | tf_op jit(solution)/shard_map/caption_two/pallas_call | solution.py:399
  58.3 2.1 %collective-permute-start.6 = (bf16[16,128,128]{2,1,0:T(8,128)(2,1)S(1)}, bf16[16,128,128]{2,1,0:T(8,128)(2,1)S(1)}, u32[]{:S(2)}, u32[]{:S(2)}) collective-permute-start(bf16[16,128,128]{2,1,0:T(8,128)(2,1)S(1)} %get-tuple-element.38), channel_id=1, source_target_pairs={{0,4},{4,0},{8,12},{12,8},{16,20},{20,16},{24,28},{28,24},{1,5},{5... | collective-permute-start | bytes 1572872 | tf_op jit(solution)/shard_map/ppermute | solution.py:22
  60.4 5.9 %collective-permute-start.9 = (bf16[16,128,128]{2,1,0:T(8,128)(2,1)S(1)}, bf16[16,128,128]{2,1,0:T(8,128)(2,1)S(1)}, u32[]{:S(2)}, u32[]{:S(2)}) collective-permute-start(bf16[16,128,128]{2,1,0:T(8,128)(2,1)S(1)} %get-tuple-element.40), channel_id=1, source_target_pairs={{0,8},{4,12},{8,0},{12,4},{16,24},{20,28},{24,16},{28,20},{1,9},{5... | collective-permute-start | bytes 1572872 | tf_op jit(solution)/shard_map/ppermute | solution.py:22
  66.3 1.9 %fusion = f32[128,128]{1,0:T(8,128)S(1)} fusion(f32[128,128]{1,0:T(8,128)S(1)} %convolution_bitcast_fusion.1, f32[16,128,128]{2,1,0:T(8,128)S(1)} %get-tuple-element.35), kind=kOutput, calls=%fused_computation.3 | convolution fusion | flops 402669568 | bytes 1179648 | tf_op jit(solution)/shard_map/dot_general | solution.py:548
  68.2 1.4 collective-permute-start.5
  69.5 0.9 collective-permute-done.5
  70.5 7.7 %collective-permute-done.9 = bf16[16,128,128]{2,1,0:T(8,128)(2,1)S(1)} collective-permute-done((bf16[16,128,128]{2,1,0:T(8,128)(2,1)S(1)}, bf16[16,128,128]{2,1,0:T(8,128)(2,1)S(1)}, u32[]{:S(2)}, u32[]{:S(2)}) %collective-permute-start.9) | collective-permute-done | bytes 524320 | tf_op jit(solution)/shard_map/ppermute | solution.py:22
  78.5 2.4 %collective-permute-start.7 = (bf16[10,128,128]{2,1,0:T(8,128)(2,1)S(1)}, bf16[10,128,128]{2,1,0:T(8,128)(2,1)S(1)}, u32[]{:S(2)}, u32[]{:S(2)}) collective-permute-start(bf16[10,128,128]{2,1,0:T(8,128)(2,1)S(1)} %pad_maximum_fusion.2), channel_id=1, source_target_pairs={{0,8},{4,12},{8,0},{12,4},{16,24},{20,28},{24,16},{28,20},{1,9},{5... | collective-permute-start | bytes 983048 | tf_op jit(solution)/shard_map/ppermute | solution.py:22
  80.9 6.3 %collective-permute-done.10 = bf16[8,128,128]{2,1,0:T(8,128)(2,1)S(1)} collective-permute-done((bf16[8,128,128]{2,1,0:T(8,128)(2,1)S(1)}, bf16[8,128,128]{2,1,0:T(8,128)(2,1)S(1)}, u32[]{:S(2)}, u32[]{:S(2)}) %collective-permute-start.10) | collective-permute-done | bytes 262176 | tf_op jit(solution)/shard_map/ppermute | solution.py:22
  87.4 4.8 %collective-permute-start.11 = (bf16[8,128,128]{2,1,0:T(8,128)(2,1)S(1)}, bf16[8,128,128]{2,1,0:T(8,128)(2,1)S(1)}, u32[]{:S(2)}, u32[]{:S(2)}) collective-permute-start(bf16[8,128,128]{2,1,0:T(8,128)(2,1)S(1)} %reduce-precision_convert_fusion.4), channel_id=1, source_target_pairs={{0,16},{4,20},{8,24},{12,28},{16,0},{20,4},{24,8},{28,12},{1,17},{... | collective-permute-start | bytes 786440 | tf_op jit(solution)/shard_map/ppermute | solution.py:22
  92.3 1.6 %collective-permute-start.8 = (bf16[10,128,128]{2,1,0:T(8,128)(2,1)S(1)}, bf16[10,128,128]{2,1,0:T(8,128)(2,1)S(1)}, u32[]{:S(2)}, u32[]{:S(2)}) collective-permute-start(bf16[10,128,128]{2,1,0:T(8,128)(2,1)S(1)} %pad_maximum_fusion.3), channel_id=1, source_target_pairs={{0,16},{4,20},{8,24},{12,28},{16,0},{20,4},{24,8},{28,12},{1,17},{... | collective-permute-start | bytes 983048 | tf_op jit(solution)/shard_map/ppermute | solution.py:22
  94.0 17.3 %collective-permute-done.11 = bf16[8,128,128]{2,1,0:T(8,128)(2,1)S(1)} collective-permute-done((bf16[8,128,128]{2,1,0:T(8,128)(2,1)S(1)}, bf16[8,128,128]{2,1,0:T(8,128)(2,1)S(1)}, u32[]{:S(2)}, u32[]{:S(2)}) %collective-permute-start.11) | collective-permute-done | bytes 262176 | tf_op jit(solution)/shard_map/ppermute | solution.py:22
  111.6 6.6 %collective-permute-done.8 = bf16[10,128,128]{2,1,0:T(8,128)(2,1)S(1)} collective-permute-done((bf16[10,128,128]{2,1,0:T(8,128)(2,1)S(1)}, bf16[10,128,128]{2,1,0:T(8,128)(2,1)S(1)}, u32[]{:S(2)}, u32[]{:S(2)}) %collective-permute-start.8) | collective-permute-done | bytes 327712 | tf_op jit(solution)/shard_map/ppermute | solution.py:22
  119.1 7.5 %collective-permute-done.13 = bf16[8,128,128]{2,1,0:T(8,128)(2,1)S(1)} collective-permute-done((bf16[8,128,128]{2,1,0:T(8,128)(2,1)S(1)}, bf16[8,128,128]{2,1,0:T(8,128)(2,1)S(1)}, u32[]{:S(2)}, u32[]{:S(2)}) %collective-permute-start.13) | collective-permute-done | bytes 262176 | tf_op jit(solution)/shard_map/ppermute | solution.py:22
  126.9 1.3 collective-permute-done.12
  128.3 2.6 %collective-permute-start.15 = (bf16[16,128,128]{2,1,0:T(8,128)(2,1)S(1)}, bf16[16,128,128]{2,1,0:T(8,128)(2,1)S(1)}, u32[]{:S(2)}, u32[]{:S(2)}) collective-permute-start(bf16[16,128,128]{2,1,0:T(8,128)(2,1)S(1)} %maximum_select_fusion.3), channel_id=1, source_target_pairs={{0,8},{4,12},{8,0},{12,4},{16,24},{20,28},{24,16},{28,20},{1,9},{5... | collective-permute-start | bytes 1572872 | tf_op jit(solution)/shard_map/ppermute | solution.py:22
  130.9 0.7 convert_add_fusion.gram
  131.6 10.0 %factorize.1 = (f32[128,128]{1,0:T(8,128)}, f32[128,128]{1,0:T(8,128)}) custom-call(f32[128,128]{1,0:T(8,128)} %convert_add_fusion.gram), custom_call_target="tpu_custom_call" | custom-call | tf_op jit(solution)/shard_map/factorize/pallas_call | solution.py:424
  141.6 2.8 %fusion.19 = f32[2048,128]{1,0:T(8,128)} fusion(f32[2048,128]{1,0:T(8,128)S(1)} %bitcast.72, f32[128,128]{1,0:T(8,128)} %get-tuple-element.41), kind=kOutput, calls=%fused_computation.65 | convolution fusion | flops 402653184 | bytes 2162688 | tf_op jit(solution)/shard_map/dot_general | solution.py:591
  144.7 1.5 %pad_maximum_fusion = bf16[64,128,128]{2,1,0:T(8,128)(2,1)} fusion(bf16[32,128,128]{2,1,0:T(8,128)(2,1)S(1)} %maximum_select_fusion.1, bf16[32,128,128]{2,1,0:T(8,128)(2,1)S(1)} %maximum_select_fusion), kind=kLoop, calls=%fused_computation | loop fusion | flops 1048576 | bytes 4194304 | tf_op jit(solution)/shard_map/concatenate | solution.py:582
  (54 shorter events, 3.9 us)
Async XLA Ops:
  13.8 2.7 %collective-permute-start = (bf16[32,128,128]{2,1,0:T(8,128)(2,1)S(1)}, bf16[32,128,128]{2,1,0:T(8,128)(2,1)S(1)}, u32[]{:S(2)}, u32[]{:S(2)}) collective-permute-start(bf16[32,128,128]{2,1,0:T(8,128)(2,1)S(1)} %get-tuple-element.24), channel_id=1, source_target_pairs={{0,1},{1,0},{2,3},{3,2},{4,5},{5,4},{6,7},{7,6},{8,9},{9,8},{10,11... | collective-permute-start | bytes 3145736 | tf_op jit(solution)/shard_map/ppermute | solution.py:22
  16.6 3.8 %copy-start.1 = (s32[1,640]{1,0:T(1,128)S(1)}, s32[1,640]{1,0:T(1,128)}, u32[]{:S(2)}) copy-start(s32[1,640]{1,0:T(1,128)} %rows.1) | copy-start | bytes 7684
  16.6 3.8 %copy-start.2 = (s32[1,640]{1,0:T(1,128)S(1)}, s32[1,640]{1,0:T(1,128)}, u32[]{:S(2)}) copy-start(s32[1,640]{1,0:T(1,128)} %cols.1) | copy-start | bytes 7684
  16.6 5.6 %copy-start.4 = (f32[8192]{0:T(1024)S(1)}, f32[8192]{0:T(1024)}, u32[]{:S(2)}) copy-start(f32[8192]{0:T(1024)} %param.11) | copy-start | bytes 98308
  16.9 15.7 %collective-permute-start.1 = (bf16[16,128,128]{2,1,0:T(8,128)(2,1)S(1)}, bf16[16,128,128]{2,1,0:T(8,128)(2,1)S(1)}, u32[]{:S(2)}, u32[]{:S(2)}) collective-permute-start(bf16[16,128,128]{2,1,0:T(8,128)(2,1)S(1)} %get-tuple-element.50), channel_id=1, source_target_pairs={{0,2},{1,3},{2,0},{3,1},{4,6},{5,7},{6,4},{7,5},{8,10},{9,11},{10,... | collective-permute-start | bytes 1572872 | tf_op jit(solution)/shard_map/ppermute | solution.py:22
  32.9 3.8 %collective-permute-start.2 = (bf16[16,128,128]{2,1,0:T(8,128)(2,1)S(1)}, bf16[16,128,128]{2,1,0:T(8,128)(2,1)S(1)}, u32[]{:S(2)}, u32[]{:S(2)}) collective-permute-start(bf16[16,128,128]{2,1,0:T(8,128)(2,1)S(1)} %get-tuple-element.45.mine), channel_id=1, source_target_pairs={{0,1},{1,0},{2,3},{3,2},{4,5},{5,4},{6,7},{7,6},{8,9},{9,8},{10,11... | collective-permute-start | bytes 1572872 | tf_op jit(solution)/shard_map/ppermute | solution.py:22
  33.0 14.3 %collective-permute-start.3 = (bf16[16,128,128]{2,1,0:T(8,128)(2,1)S(1)}, bf16[16,128,128]{2,1,0:T(8,128)(2,1)S(1)}, u32[]{:S(2)}, u32[]{:S(2)}) collective-permute-start(bf16[16,128,128]{2,1,0:T(8,128)(2,1)S(1)} %get-tuple-element.49), channel_id=1, source_target_pairs={{0,2},{1,3},{2,0},{3,1},{4,6},{5,7},{6,4},{7,5},{8,10},{9,11},{10,... | collective-permute-start | bytes 1572872 | tf_op jit(solution)/shard_map/ppermute | solution.py:22
  42.4 2.0 %copy-start = (f32[65,128,128]{2,1,0:T(8,128)}, f32[65,128,128]{2,1,0:T(8,128)S(1)}, u32[]{:S(2)}) copy-start(f32[65,128,128]{2,1,0:T(8,128)S(1)} %get-tuple-element.29.before_h) | copy-start | bytes 12779524
  44.4 4.4 %copy-start.3 = (f32[8192]{0:T(1024)S(1)}, f32[8192]{0:T(1024)}, u32[]{:S(2)}) copy-start(f32[8192]{0:T(1024)} %param.12) | copy-start | bytes 98308
  47.7 2.6 %collective-permute-start.4 = (bf16[16,128,128]{2,1,0:T(8,128)(2,1)S(1)}, bf16[16,128,128]{2,1,0:T(8,128)(2,1)S(1)}, u32[]{:S(2)}, u32[]{:S(2)}) collective-permute-start(bf16[16,128,128]{2,1,0:T(8,128)(2,1)S(1)} %get-tuple-element.48.mine), channel_id=1, source_target_pairs={{0,1},{1,0},{2,3},{3,2},{4,5},{5,4},{6,7},{7,6},{8,9},{9,8},{10,11... | collective-permute-start | bytes 1572872 | tf_op jit(solution)/shard_map/ppermute | solution.py:22
  58.3 20.1 %collective-permute-start.6 = (bf16[16,128,128]{2,1,0:T(8,128)(2,1)S(1)}, bf16[16,128,128]{2,1,0:T(8,128)(2,1)S(1)}, u32[]{:S(2)}, u32[]{:S(2)}) collective-permute-start(bf16[16,128,128]{2,1,0:T(8,128)(2,1)S(1)} %get-tuple-element.38), channel_id=1, source_target_pairs={{0,4},{4,0},{8,12},{12,8},{16,20},{20,16},{24,28},{28,24},{1,5},{5... | collective-permute-start | bytes 1572872 | tf_op jit(solution)/shard_map/ppermute | solution.py:22
  60.4 17.8 %collective-permute-start.9 = (bf16[16,128,128]{2,1,0:T(8,128)(2,1)S(1)}, bf16[16,128,128]{2,1,0:T(8,128)(2,1)S(1)}, u32[]{:S(2)}, u32[]{:S(2)}) collective-permute-start(bf16[16,128,128]{2,1,0:T(8,128)(2,1)S(1)} %get-tuple-element.40), channel_id=1, source_target_pairs={{0,8},{4,12},{8,0},{12,4},{16,24},{20,28},{24,16},{28,20},{1,9},{5... | collective-permute-start | bytes 1572872 | tf_op jit(solution)/shard_map/ppermute | solution.py:22
  68.2 2.3 %collective-permute-start.5 = (f32[128,128]{1,0:T(8,128)S(1)}, f32[128,128]{1,0:T(8,128)S(1)}, u32[]{:S(2)}, u32[]{:S(2)}) collective-permute-start(f32[128,128]{1,0:T(8,128)S(1)} %fusion), channel_id=1, source_target_pairs={{0,1},{1,0},{2,3},{3,2},{4,5},{5,4},{6,7},{7,6},{8,9},{9,8},{10,11... | collective-permute-start | bytes 196616 | tf_op jit(solution)/shard_map/ppermute | solution.py:22
  78.3 9.0 %collective-permute-start.10 = (bf16[8,128,128]{2,1,0:T(8,128)(2,1)S(1)}, bf16[8,128,128]{2,1,0:T(8,128)(2,1)S(1)}, u32[]{:S(2)}, u32[]{:S(2)}) collective-permute-start(bf16[8,128,128]{2,1,0:T(8,128)(2,1)S(1)} %reduce-precision_convert_fusion.5), channel_id=1, source_target_pairs={{0,4},{4,0},{8,12},{12,8},{16,20},{20,16},{24,28},{28,24},{1,5},{5... | collective-permute-start | bytes 786440 | tf_op jit(solution)/shard_map/ppermute | solution.py:22
  78.5 13.6 %collective-permute-start.7 = (bf16[10,128,128]{2,1,0:T(8,128)(2,1)S(1)}, bf16[10,128,128]{2,1,0:T(8,128)(2,1)S(1)}, u32[]{:S(2)}, u32[]{:S(2)}) collective-permute-start(bf16[10,128,128]{2,1,0:T(8,128)(2,1)S(1)} %pad_maximum_fusion.2), channel_id=1, source_target_pairs={{0,8},{4,12},{8,0},{12,4},{16,24},{20,28},{24,16},{28,20},{1,9},{5... | collective-permute-start | bytes 983048 | tf_op jit(solution)/shard_map/ppermute | solution.py:22
  87.4 24.0 %collective-permute-start.11 = (bf16[8,128,128]{2,1,0:T(8,128)(2,1)S(1)}, bf16[8,128,128]{2,1,0:T(8,128)(2,1)S(1)}, u32[]{:S(2)}, u32[]{:S(2)}) collective-permute-start(bf16[8,128,128]{2,1,0:T(8,128)(2,1)S(1)} %reduce-precision_convert_fusion.4), channel_id=1, source_target_pairs={{0,16},{4,20},{8,24},{12,28},{16,0},{20,4},{24,8},{28,12},{1,17},{... | collective-permute-start | bytes 786440 | tf_op jit(solution)/shard_map/ppermute | solution.py:22
  92.3 25.9 %collective-permute-start.8 = (bf16[10,128,128]{2,1,0:T(8,128)(2,1)S(1)}, bf16[10,128,128]{2,1,0:T(8,128)(2,1)S(1)}, u32[]{:S(2)}, u32[]{:S(2)}) collective-permute-start(bf16[10,128,128]{2,1,0:T(8,128)(2,1)S(1)} %pad_maximum_fusion.3), channel_id=1, source_target_pairs={{0,16},{4,20},{8,24},{12,28},{16,0},{20,4},{24,8},{28,12},{1,17},{... | collective-permute-start | bytes 983048 | tf_op jit(solution)/shard_map/ppermute | solution.py:22
  118.4 8.2 %collective-permute-start.13 = (bf16[8,128,128]{2,1,0:T(8,128)(2,1)S(1)}, bf16[8,128,128]{2,1,0:T(8,128)(2,1)S(1)}, u32[]{:S(2)}, u32[]{:S(2)}) collective-permute-start(bf16[8,128,128]{2,1,0:T(8,128)(2,1)S(1)} %multiply_convert_fusion.2), channel_id=1, source_target_pairs={{0,8},{4,12},{8,0},{12,4},{16,24},{20,28},{24,16},{28,20},{1,9},{5... | collective-permute-start | bytes 786440 | tf_op jit(solution)/shard_map/ppermute | solution.py:22
  118.6 9.6 %collective-permute-start.12 = (bf16[10,128,128]{2,1,0:T(8,128)(2,1)S(1)}, bf16[10,128,128]{2,1,0:T(8,128)(2,1)S(1)}, u32[]{:S(2)}, u32[]{:S(2)}) collective-permute-start(bf16[10,128,128]{2,1,0:T(8,128)(2,1)S(1)} %pad_maximum_fusion.4), channel_id=1, source_target_pairs={{0,4},{4,0},{8,12},{12,8},{16,20},{20,16},{24,28},{28,24},{1,5},{5... | collective-permute-start | bytes 983048 | tf_op jit(solution)/shard_map/ppermute | solution.py:22
  126.7 17.7 %collective-permute-start.14 = (bf16[16,128,128]{2,1,0:T(8,128)(2,1)S(1)}, bf16[16,128,128]{2,1,0:T(8,128)(2,1)S(1)}, u32[]{:S(2)}, u32[]{:S(2)}) collective-permute-start(bf16[16,128,128]{2,1,0:T(8,128)(2,1)S(1)} %maximum_select_fusion.2), channel_id=1, source_target_pairs={{0,4},{4,0},{8,12},{12,8},{16,20},{20,16},{24,28},{28,24},{1,5},{5... | collective-permute-start | bytes 1572872 | tf_op jit(solution)/shard_map/ppermute | solution.py:22
  128.3 16.2 %collective-permute-start.15 = (bf16[16,128,128]{2,1,0:T(8,128)(2,1)S(1)}, bf16[16,128,128]{2,1,0:T(8,128)(2,1)S(1)}, u32[]{:S(2)}, u32[]{:S(2)}) collective-permute-start(bf16[16,128,128]{2,1,0:T(8,128)(2,1)S(1)} %maximum_select_fusion.3), channel_id=1, source_target_pairs={{0,8},{4,12},{8,0},{12,4},{16,24},{20,28},{24,16},{28,20},{1,9},{5... | collective-permute-start | bytes 1572872 | tf_op jit(solution)/shard_map/ppermute | solution.py:22

commit v3 on v2

--- a/solution.py
+++ b/solution.py
@@ -90,43 +90,42 @@
         lax.fori_loop(0, size, block, 0, unroll=2)
 
 
-def fetch(order, first, tiles, held, sem, chunk):
+def fetch_one(order, tiles, held, sem, chunk, j):
+    slot = lax.rem(chunk, sem.shape[0])
+    tile = order[0, chunk * 2 * UNROLL + j]
+    pltpu.make_async_copy(tiles.at[tile], held.at[slot * 2 * UNROLL + j], sem.at[slot]).start()
+
+
+def multiply(transposed, order, pairs, dead, tiles, held, sem, panel, acc, meanwhile):
     slots = sem.shape[0]
-    slot = lax.rem(chunk, slots)
-    for j in range(2 * UNROLL):
-        tile = order[0, first + chunk * 2 * UNROLL + j]
-        pltpu.make_async_copy(tiles.at[tile], held.at[slot * 2 * UNROLL + j], sem.at[slot]).start()
-
-
-def multiply(transposed, order, first, pairs, dead, tiles, held, sem, panel, acc, ahead=lambda: None):
-    slots = sem.shape[0]
-    chunks = pl.cdiv(pairs, UNROLL)
-
-    def begin(chunk, carry):
-        fetch(order, first, tiles, held, sem, chunk)
-        return carry
-
-    lax.fori_loop(0, jnp.minimum(chunks, slots), begin, 0)
-    ahead()
-
-    def work(chunk, carry):
+    ahead = slots - 1
+    chunks = jnp.maximum(pl.cdiv(pairs, UNROLL), ahead)
+    starts = ahead * 2 * UNROLL
+    done = 0
+    for i in range(starts):
+        fetch_one(order, tiles, held, sem, i // (2 * UNROLL), i % (2 * UNROLL))
+        while done * starts < (i + 1) * len(meanwhile):
+            meanwhile[done]()
+            done += 1
+
+    def work(more, chunk, carry):
         slot = lax.rem(chunk, slots)
         whole = pl.ds(slot * 2 * UNROLL, 2 * UNROLL)
         pltpu.make_async_copy(tiles.at[pl.ds(0, 2 * UNROLL)], held.at[whole], sem.at[slot]).wait()
         for j in range(UNROLL):
+            if more:
+                for k in (2 * j, 2 * j + 1):
+                    fetch_one(order, tiles, held, sem, chunk + ahead, k)
             q = chunk * UNROLL + j
-            p = first + 2 * q
+            p = 2 * q
             h = slot * 2 * UNROLL + 2 * j
             to = jnp.where(q < pairs, order[2, p], dead)
             add_pair(transposed, held, (h, h + 1), panel, (order[1, p], order[1, p + 1]), acc, to)
-
-        @pl.when(chunk + slots < chunks)
-        def _():
-            fetch(order, first, tiles, held, sem, chunk + slots)
-
         return carry
 
-    lax.fori_loop(0, chunks, work, 0)
+    steady = chunks - ahead
+    lax.fori_loop(0, steady, functools.partial(work, True), 0)
+    lax.fori_loop(steady, chunks, functools.partial(work, False), 0)
 
 
 def shares_of(row, share):
@@ -176,15 +175,16 @@
     acc[...] = jnp.zeros_like(acc)
     order_copy.wait()
 
-    def ahead():
-        copies[2].wait()
-        copies[3].wait()
-        scale = lax.transpose(lax.rsqrt(degree[...]), (1, 0))
-        for g in range(groups):
-            panel[g] = (panel[g].astype(F32) * scale[:, g : g + 1]).astype(BF16)
-        panel[groups] = jnp.zeros(panel.shape[1:], BF16)
-
-    multiply(False, order_s, 0, order_s[3, 0], groups, tiles, held, tile_sem, panel, acc, ahead)
+    copies[2].wait()
+    copies[3].wait()
+    scale = lax.transpose(lax.rsqrt(degree[...]), (1, 0))
+
+    def scale_block(g):
+        panel[g] = (panel[g].astype(F32) * scale[:, g : g + 1]).astype(BF16)
+
+    panel[groups] = jnp.zeros(panel.shape[1:], BF16)
+    steps = [functools.partial(scale_block, g) for g in range(groups)]
+    multiply(False, order_s, order_s[3, 0], groups, tiles, held, tile_sem, panel, acc, steps)
     split_out(acc, 0, shares, cut, core, own_one, send.at[pl.ds(0, own_one.shape[0])])
     split_out(
         acc, shares * cut, shares, share - cut, core, own_two,
@@ -212,57 +212,51 @@
         out[...] = pack_rows(order_rows(found, taken, padded, blocks, groups), places)
 
 
-def caption_part(order, tiles, mine, other, acc, panel, held, sem, tile_sem, fill):
+def caption_part(order, tiles, mine, other, acc, panel, held, sem, tile_sem):
     half = mine.shape[0]
     copies = [
         pltpu.make_async_copy(source, panel.at[pl.ds(i * half, half)], sem.at[i])
         for i, source in enumerate((mine, other))
     ]
-
-    def ahead():
-        for copy in copies:
-            copy.start()
-        panel[2 * half] = jnp.zeros(panel.shape[1:], BF16)
-        fill()
-        for copy in copies:
-            copy.wait()
-
-    multiply(
-        True, order, 0, order[3, 0], acc.shape[0] - 1, tiles, held, tile_sem, panel, acc, ahead
-    )
-
-
-def third_kernel(order, tiles, mine, other, acc, mark, panel, held, sem, tile_sem):
+    for copy in copies:
+        copy.start()
+    panel[2 * half] = jnp.zeros(panel.shape[1:], BF16)
+
+    def clear(g):
+        acc[g] = jnp.zeros(acc.shape[1:], F32)
+
+    steps = [functools.partial(clear, g) for g in range(acc.shape[0])]
+    steps += [copy.wait for copy in copies]
+    dead = acc.shape[0] - 1
+    multiply(True, order, order[3, 0], dead, tiles, held, tile_sem, panel, acc, steps)
+
+
+def third_kernel(order, tiles, mine, other, out, mark, acc, panel, held, sem, tile_sem):
     mark[...] = jnp.zeros_like(mark)
-
-    def fill():
-        acc[...] = jnp.zeros_like(acc)
-
-    caption_part(order, tiles, mine, other, acc, panel, held, sem, tile_sem, fill)
+    caption_part(order, tiles, mine, other, acc, panel, held, sem, tile_sem)
+
+    def block(i, carry):
+        out[i] = acc[i].astype(BF16)
+        return carry
+
+    lax.fori_loop(0, out.shape[0], block, 0, unroll=4)
 
 
 def fourth_kernel(
-    meta, order, tiles, before_h, mine, other, own_a, send_a, own_b, send_b,
-    acc, before, panel, held, sem, before_sem, tile_sem,
+    meta, order, tiles, before, mine, other, own_a, send_a, own_b, send_b,
+    acc, panel, held, sem, tile_sem,
 ):
-    copy = pltpu.make_async_copy(before_h, before, before_sem)
-    copy.start()
-
-    def fill():
-        acc[...] = jnp.zeros_like(acc)
-
-    caption_part(order, tiles, mine, other, acc, panel, held, sem, tile_sem, fill)
-    copy.wait()
+    caption_part(order, tiles, mine, other, acc, panel, held, sem, tile_sem)
     part = own_a.shape[0]
     for own, send, base, bit in ((own_a, send_a, 0, meta[0]), (own_b, send_b, 2 * part, meta[1])):
 
         def block(i, carry):
             keep, give = base + bit * part + i, base + (1 - bit) * part + i
-            own[i] = acc[keep] + before[keep]
-            send[i] = (acc[give] + before[give]).astype(BF16)
+            own[i] = acc[keep] + before[keep].astype(F32)
+            send[i] = (acc[give] + before[give].astype(F32)).astype(BF16)
             return carry
 
-        lax.fori_loop(0, part, block, 0, unroll=2)
+        lax.fori_loop(0, part, block, 0, unroll=4)
 
 
 def factor_kernel(root, gram, upper, inverse, rest, left):
@@ -277,8 +271,9 @@
         scale = jnp.zeros((8, size), F32)
         for s in range(8):
             pivot = columns[s][s : s + 1]
-            scale = jnp.where(row == s, lax.rsqrt(pivot), scale)
-            f = jnp.where(row > s, columns[s] / pivot, 0.0)
+            root_of = lax.rsqrt(pivot)
+            scale = jnp.where(row == s, root_of, scale)
+            f = jnp.where(row > s, columns[s] * (root_of * root_of), 0.0)
             for k in range(s + 1, 8):
                 columns[k] = columns[k] - f * columns[k][s : s + 1]
             u = u - f * u[s : s + 1]
@@ -304,7 +299,7 @@
 ANY = pl.BlockSpec(memory_space=pl.ANY)
 HBM = pl.BlockSpec(memory_space=pltpu.HBM)
 PARAMS = pltpu.CompilerParams(vmem_limit_bytes=32 * 2**20)
-DEPTH = 4
+DEPTH = 3
 
 
 def in_hbm(x):
@@ -377,10 +372,11 @@
         in_specs=[SMEM, HBM, ANY, ANY],
         out_specs=[VMEM] * 2,
         out_shape=[
-            jax.ShapeDtypeStruct((groups + 1, *block), F32),
+            jax.ShapeDtypeStruct((groups, *block), BF16),
             jax.ShapeDtypeStruct((1, 128), F32),
         ],
         scratch_shapes=[
+            pltpu.VMEM((groups + 1, *block), F32),
             pltpu.VMEM((2 * mine.shape[0] + 1, *block), BF16),
             held,
             pltpu.SemaphoreType.DMA((2,)),
@@ -395,10 +391,9 @@
     block = mine.shape[1:]
     part = groups // 4
     held, tile_sem = buffers(block[0])
-    total = pltpu.VMEM((groups + 1, *block), F32)
     return pl.pallas_call(
         fourth_kernel,
-        in_specs=[SMEM, SMEM, HBM, HBM, ANY, ANY],
+        in_specs=[SMEM, SMEM, HBM, VMEM, ANY, ANY],
         out_specs=[VMEM] * 4,
         out_shape=[
             jax.ShapeDtypeStruct((part, *block), F32),
@@ -406,17 +401,15 @@
         ]
         * 2,
         scratch_shapes=[
-            total,
-            total,
+            pltpu.VMEM((groups + 1, *block), F32),
             pltpu.VMEM((2 * mine.shape[0] + 1, *block), BF16),
             held,
             pltpu.SemaphoreType.DMA((2,)),
-            pltpu.SemaphoreType.DMA,
             tile_sem,
         ],
         compiler_params=PARAMS,
         name="caption_two",
-    )(meta, order, in_hbm(tiles), in_hbm(before), mine, other)
+    )(meta, order, in_hbm(tiles), before, mine, other)
 
 
 def factorize(gram, root):
@@ -545,7 +538,7 @@
 
     def products(image):
         flat = image.reshape(-1, width)
-        return jnp.dot(flat.T, flat, precision=lax.Precision.HIGHEST, preferred_element_type=F32)
+        return jnp.dot(flat.T, flat, precision=lax.Precision.HIGH, preferred_element_type=F32)
 
     scale_one, scale_two = row_scale[:, :cut], row_scale[:, cut:]
     order_one, scale_one = lax.optimization_barrier((order_one, scale_one))
@@ -592,7 +585,7 @@
         rows,
         inverse,
         (((1,), (1,)), ((), ())),
-        precision=lax.Precision.HIGHEST,
+        precision=lax.Precision.HIGH,
         preferred_element_type=F32,
     )
     return (basis, factor, next_panel)

time: 145 us -> 141 us (0.972); the launches traced: 146 us -> 139 us
  starting transfers between devices: 28 us -> 10.7 us
  Pallas kernels: 37.9 us -> 48.3 us
  waiting for transfers between devices: 65 us -> 67.1 us
  matrix products: 6.53 us -> 4.46 us
  local copies, waits for them, and re-layouts: 2.13 us -> 0.51 us
    ppermute x16, starting transfers between devices: 28 us -> 10.7 us  [swap(): lax.ppermute(row_major(x), axis, [(i, i ^ 1 << bit) for i in range(n)])]
    pallas_call x1, Pallas kernels: 5.68 us -> 10.4 us  [backward_one(): pl.pallas_call(third_kernel, in_specs=[SMEM, HBM, ANY, ANY], out_specs=[V...]
    pallas_call x1, Pallas kernels: 12.5 us -> 16.2 us  [forward(): pl.pallas_call(functools.partial(image_kernel, shares, cut), in_specs=[SM...]
    ppermute x16, waiting for transfers between devices: 65 us -> 67.1 us  [swap(): lax.ppermute(row_major(x), axis, [(i, i ^ 1 << bit) for i in range(n)])]
    pallas_call x1, Pallas kernels: 7.96 us -> 9.88 us  [backward_two(): pl.pallas_call(fourth_kernel, in_specs=[SMEM, SMEM, HBM, VMEM, ANY, ANY],...]
    dot_general x2, matrix products: 3.73 us -> 2.06 us  [products(): jnp.dot(flat.T, flat, precision=lax.Precision.HIGH, preferred_element_typ...]
    unnamed x10 -> x14, local copies, waits for them, and re-layouts: 1.99 us -> 0.37 us
  transfers between devices with their start and end apart: 16 -> 16, of which waited for: 11 -> 12; matrix products, arithmetic and copies ran while one was open for 6% -> 5% of each run, Pallas kernels for 12% -> 16%
where the time goes in v3:
time: 141 us; the launch traced here: 139 us
  waiting for transfers between devices  67.1 us (48%)
  Pallas kernels  48.3 us (34%)
  starting transfers between devices  10.7 us (8%)
  other arithmetic  5.93 us (4%)
  matrix products  4.46 us (3%)
  between operations  1.65 us (1%)
    ppermute x16, waiting for transfers between devices, swap(): lax.ppermute(row_major(x), axis, [(i, i ^ 1 << bit) for i in range(n)])  67.1 us
    pallas_call x1, Pallas kernels, forward(): pl.pallas_call(functools.partial(image_kernel, shares, cut), in_specs=[SM...  16.2 us
    ppermute x16, starting transfers between devices, swap(): lax.ppermute(row_major(x), axis, [(i, i ^ 1 << bit) for i in range(n)])  10.7 us
    pallas_call x1, Pallas kernels, backward_one(): pl.pallas_call(third_kernel, in_specs=[SMEM, HBM, ANY, ANY], out_specs=[V...  10.4 us
    pallas_call x1, Pallas kernels, factorize(): pl.pallas_call(functools.partial(factor_kernel, root), in_specs=[VMEM], o...  9.97 us
    pallas_call x1, Pallas kernels, backward_two(): pl.pallas_call(fourth_kernel, in_specs=[SMEM, SMEM, HBM, VMEM, ANY, ANY],...  9.88 us
  transfers between devices with their start and end apart: 16, of which 12 were waited for; matrix products, arithmetic and copies ran while one was open for 5% of the time, Pallas kernels for 16%

profile of v3, /device:TPU:0, one launch (start us, length us, event | category | flops | bytes accessed | tf_op | source)
XLA Modules:
  0.0 138.6 jit_solution(16679810729622700293)
XLA Ops:
  1.4 16.2 %image.1 = (f32[16,128,128]{2,1,0:T(8,128)S(1)}, f32[16,128,128]{2,1,0:T(8,128)S(1)}, bf16[32,128,128]{2,1,0:T(8,128)(2,1)S(1)}) custom-call(s32[2]{0:T(128)S(1)} %pad_add_fusion.meta, s32[1,640]{1,0:T(1,128)} %rows.1, s32[1,640]{1,0:T(1,128)} %cols.1, f32[64,128]{1,0:T(8,128)} %bitcast.75, bf16[64,128,128]{2,1,0:T(8,128)(2,1)} %bitcast.74, ...), custom_call_target="tpu_custom_call" | custom-call | tf_op jit(solution)/shard_map/image/pallas_call | solution.py:328
  17.7 2.6 %collective-permute-done = bf16[32,128,128]{2,1,0:T(8,128)(2,1)S(1)} collective-permute-done((bf16[32,128,128]{2,1,0:T(8,128)(2,1)S(1)}, bf16[32,128,128]{2,1,0:T(8,128)(2,1)S(1)}, u32[]{:S(2)}, u32[]{:S(2)}) %collective-permute-start) | collective-permute-done | bytes 1048608 | tf_op jit(solution)/shard_map/ppermute | solution.py:22
  21.0 1.8 %orders.1 = (s32[8,768]{1,0:T(8,128)S(1)}, s32[8,768]{1,0:T(8,128)S(1)}) custom-call(s32[2]{0:T(128)S(1)} %pad_add_fusion.meta, s32[1,640]{1,0:T(1,128)S(1)} %copy-done, s32[1,640]{1,0:T(1,128)S(1)} %copy-done.1), custom_call_target="tpu_custom_call" | custom-call | tf_op jit(solution)/shard_map/orders/pallas_call | solution.py:357
  22.9 11.7 %collective-permute-done.1 = bf16[16,128,128]{2,1,0:T(8,128)(2,1)S(1)} collective-permute-done((bf16[16,128,128]{2,1,0:T(8,128)(2,1)S(1)}, bf16[16,128,128]{2,1,0:T(8,128)(2,1)S(1)}, u32[]{:S(2)}, u32[]{:S(2)}) %collective-permute-start.1) | collective-permute-done | bytes 524320 | tf_op jit(solution)/shard_map/ppermute | solution.py:22
  34.6 0.4 multiply_convert_fusion.1
  35.1 0.4 collective-permute-start.3
  35.5 1.0 convolution_bitcast_fusion.1
  36.5 0.5 collective-permute-done.2.other
  37.0 10.4 %caption_one.1 = (bf16[64,128,128]{2,1,0:T(8,128)(2,1)S(1)}, f32[1,128]{1,0:T(1,128)S(1)}) custom-call(s32[8,768]{1,0:T(8,128)S(1)} %get-tuple-element.28.order, bf16[640,128,128]{2,1,0:T(8,128)(2,1)} %tiles.5, bf16[16,128,128]{2,1,0:T(8,128)(2,1)S(1)} %get-tuple-element.45.mine, bf16[16,128,128]{2,1,0:T(8,128)(2,1)S(1)} %collective-permute-done.2.other), custom_call_target="tpu_custom_call" | custom-call | tf_op jit(solution)/shard_map/caption_one/pallas_call | solution.py:370
  47.5 2.0 %collective-permute-done.3 = bf16[16,128,128]{2,1,0:T(8,128)(2,1)S(1)} collective-permute-done((bf16[16,128,128]{2,1,0:T(8,128)(2,1)S(1)}, bf16[16,128,128]{2,1,0:T(8,128)(2,1)S(1)}, u32[]{:S(2)}, u32[]{:S(2)}) %collective-permute-start.3) | collective-permute-done | bytes 524320 | tf_op jit(solution)/shard_map/ppermute | solution.py:22
  49.4 1.3 add_multiply_fusion
  50.9 1.8 %collective-permute-done.4.other = bf16[16,128,128]{2,1,0:T(8,128)(2,1)S(1)} collective-permute-done((bf16[16,128,128]{2,1,0:T(8,128)(2,1)S(1)}, bf16[16,128,128]{2,1,0:T(8,128)(2,1)S(1)}, u32[]{:S(2)}, u32[]{:S(2)}) %collective-permute-start.4) | collective-permute-done | bytes 524320 | tf_op jit(solution)/shard_map/ppermute | solution.py:22
  52.7 9.9 %caption_two.1 = (f32[16,128,128]{2,1,0:T(8,128)S(1)}, bf16[16,128,128]{2,1,0:T(8,128)(2,1)S(1)}, f32[16,128,128]{2,1,0:T(8,128)S(1)}, bf16[16,128,128]{2,1,0:T(8,128)(2,1)S(1)}) custom-call(s32[2]{0:T(128)S(1)} %pad_add_fusion.1.meta, s32[8,768]{1,0:T(8,128)S(1)} %get-tuple-element.27.order, bf16[640,128,128]{2,1,0:T(8,128)(2,1)} %tiles.5, ...), custom_call_target="tpu_custom_call" | custom-call | tf_op jit(solution)/shard_map/caption_two/pallas_call | solution.py:394
  62.7 1.0 fusion
  63.9 1.2 collective-permute-done.5
  65.1 10.5 %collective-permute-done.9 = bf16[16,128,128]{2,1,0:T(8,128)(2,1)S(1)} collective-permute-done((bf16[16,128,128]{2,1,0:T(8,128)(2,1)S(1)}, bf16[16,128,128]{2,1,0:T(8,128)(2,1)S(1)}, u32[]{:S(2)}, u32[]{:S(2)}) %collective-permute-start.9) | collective-permute-done | bytes 524320 | tf_op jit(solution)/shard_map/ppermute | solution.py:22
  75.7 1.7 %collective-permute-start.10 = (bf16[8,128,128]{2,1,0:T(8,128)(2,1)S(1)}, bf16[8,128,128]{2,1,0:T(8,128)(2,1)S(1)}, u32[]{:S(2)}, u32[]{:S(2)}) collective-permute-start(bf16[8,128,128]{2,1,0:T(8,128)(2,1)S(1)} %reduce-precision_convert_fusion.5), channel_id=1, source_target_pairs={{0,4},{4,0},{8,12},{12,8},{16,20},{20,16},{24,28},{28,24},{1,5},{5... | collective-permute-start | bytes 786440 | tf_op jit(solution)/shard_map/ppermute | solution.py:22
  77.6 0.3 collective-permute-start.7
  77.9 4.2 %collective-permute-done.10 = bf16[8,128,128]{2,1,0:T(8,128)(2,1)S(1)} collective-permute-done((bf16[8,128,128]{2,1,0:T(8,128)(2,1)S(1)}, bf16[8,128,128]{2,1,0:T(8,128)(2,1)S(1)}, u32[]{:S(2)}, u32[]{:S(2)}) %collective-permute-start.10) | collective-permute-done | bytes 262176 | tf_op jit(solution)/shard_map/ppermute | solution.py:22
  82.3 4.2 %collective-permute-start.11 = (bf16[8,128,128]{2,1,0:T(8,128)(2,1)S(1)}, bf16[8,128,128]{2,1,0:T(8,128)(2,1)S(1)}, u32[]{:S(2)}, u32[]{:S(2)}) collective-permute-start(bf16[8,128,128]{2,1,0:T(8,128)(2,1)S(1)} %reduce-precision_convert_fusion.4), channel_id=1, source_target_pairs={{0,16},{4,20},{8,24},{12,28},{16,0},{20,4},{24,8},{28,12},{1,17},{... | collective-permute-start | bytes 786440 | tf_op jit(solution)/shard_map/ppermute | solution.py:22
  86.7 1.5 %collective-permute-start.8 = (bf16[10,128,128]{2,1,0:T(8,128)(2,1)S(1)}, bf16[10,128,128]{2,1,0:T(8,128)(2,1)S(1)}, u32[]{:S(2)}, u32[]{:S(2)}) collective-permute-start(bf16[10,128,128]{2,1,0:T(8,128)(2,1)S(1)} %pad_maximum_fusion.3), channel_id=1, source_target_pairs={{0,16},{4,20},{8,24},{12,28},{16,0},{20,4},{24,8},{28,12},{1,17},{... | collective-permute-start | bytes 983048 | tf_op jit(solution)/shard_map/ppermute | solution.py:22
  88.3 17.5 %collective-permute-done.11 = bf16[8,128,128]{2,1,0:T(8,128)(2,1)S(1)} collective-permute-done((bf16[8,128,128]{2,1,0:T(8,128)(2,1)S(1)}, bf16[8,128,128]{2,1,0:T(8,128)(2,1)S(1)}, u32[]{:S(2)}, u32[]{:S(2)}) %collective-permute-start.11) | collective-permute-done | bytes 262176 | tf_op jit(solution)/shard_map/ppermute | solution.py:22
  106.0 5.7 %collective-permute-done.8 = bf16[10,128,128]{2,1,0:T(8,128)(2,1)S(1)} collective-permute-done((bf16[10,128,128]{2,1,0:T(8,128)(2,1)S(1)}, bf16[10,128,128]{2,1,0:T(8,128)(2,1)S(1)}, u32[]{:S(2)}, u32[]{:S(2)}) %collective-permute-start.8) | collective-permute-done | bytes 327712 | tf_op jit(solution)/shard_map/ppermute | solution.py:22
  112.0 0.7 collective-permute-start.13
  112.8 0.7 collective-permute-start.12
  113.6 5.7 %collective-permute-done.13 = bf16[8,128,128]{2,1,0:T(8,128)(2,1)S(1)} collective-permute-done((bf16[8,128,128]{2,1,0:T(8,128)(2,1)S(1)}, bf16[8,128,128]{2,1,0:T(8,128)(2,1)S(1)}, u32[]{:S(2)}, u32[]{:S(2)}) %collective-permute-start.13) | collective-permute-done | bytes 262176 | tf_op jit(solution)/shard_map/ppermute | solution.py:22
  119.4 0.6 collective-permute-start.14
  120.0 3.5 %collective-permute-done.12 = bf16[10,128,128]{2,1,0:T(8,128)(2,1)S(1)} collective-permute-done((bf16[10,128,128]{2,1,0:T(8,128)(2,1)S(1)}, bf16[10,128,128]{2,1,0:T(8,128)(2,1)S(1)}, u32[]{:S(2)}, u32[]{:S(2)}) %collective-permute-start.12) | collective-permute-done | bytes 327712 | tf_op jit(solution)/shard_map/ppermute | solution.py:22
  123.7 0.7 convert_add_fusion.gram
  124.4 10.0 %factorize.1 = (f32[128,128]{1,0:T(8,128)}, f32[128,128]{1,0:T(8,128)}) custom-call(f32[128,128]{1,0:T(8,128)} %convert_add_fusion.gram), custom_call_target="tpu_custom_call" | custom-call | tf_op jit(solution)/shard_map/factorize/pallas_call | solution.py:417
  134.3 2.4 %fusion.19 = f32[2048,128]{1,0:T(8,128)} fusion(f32[2048,128]{1,0:T(8,128)S(1)} %bitcast.72, f32[128,128]{1,0:T(8,128)} %get-tuple-element.41), kind=kOutput, calls=%fused_computation.65 | convolution fusion | flops 201326592 | bytes 2162688 | tf_op jit(solution)/shard_map/dot_general | solution.py:584
  137.1 1.5 %pad_maximum_fusion = bf16[64,128,128]{2,1,0:T(8,128)(2,1)} fusion(bf16[32,128,128]{2,1,0:T(8,128)(2,1)S(1)} %maximum_select_fusion.1, bf16[32,128,128]{2,1,0:T(8,128)(2,1)S(1)} %maximum_select_fusion), kind=kLoop, calls=%fused_computation | loop fusion | flops 1048576 | bytes 4194304 | tf_op jit(solution)/shard_map/concatenate | solution.py:575
  (58 shorter events, 3.1 us)
Async XLA Ops:
  17.6 2.7 %collective-permute-start = (bf16[32,128,128]{2,1,0:T(8,128)(2,1)S(1)}, bf16[32,128,128]{2,1,0:T(8,128)(2,1)S(1)}, u32[]{:S(2)}, u32[]{:S(2)}) collective-permute-start(bf16[32,128,128]{2,1,0:T(8,128)(2,1)S(1)} %get-tuple-element.24), channel_id=1, source_target_pairs={{0,1},{1,0},{2,3},{3,2},{4,5},{5,4},{6,7},{7,6},{8,9},{9,8},{10,11... | collective-permute-start | bytes 3145736 | tf_op jit(solution)/shard_map/ppermute | solution.py:22
  20.3 0.7 copy-start
  20.3 0.7 copy-start.1
  20.3 2.5 %copy-start.6 = (f32[8192]{0:T(1024)S(1)}, f32[8192]{0:T(1024)}, u32[]{:S(2)}) copy-start(f32[8192]{0:T(1024)} %param.11) | copy-start | bytes 98308
  20.6 14.0 %collective-permute-start.1 = (bf16[16,128,128]{2,1,0:T(8,128)(2,1)S(1)}, bf16[16,128,128]{2,1,0:T(8,128)(2,1)S(1)}, u32[]{:S(2)}, u32[]{:S(2)}) collective-permute-start(bf16[16,128,128]{2,1,0:T(8,128)(2,1)S(1)} %get-tuple-element.50), channel_id=1, source_target_pairs={{0,2},{1,3},{2,0},{3,1},{4,6},{5,7},{6,4},{7,5},{8,10},{9,11},{10,... | collective-permute-start | bytes 1572872 | tf_op jit(solution)/shard_map/ppermute | solution.py:22
  35.0 12.4 %copy-start.2 = (f32[16,128,128]{2,1,0:T(8,128)}, f32[16,128,128]{2,1,0:T(8,128)S(1)}, u32[]{:S(2)}) copy-start(f32[16,128,128]{2,1,0:T(8,128)S(1)} %get-tuple-element.46) | copy-start | bytes 3145732
  35.0 2.0 %collective-permute-start.2 = (bf16[16,128,128]{2,1,0:T(8,128)(2,1)S(1)}, bf16[16,128,128]{2,1,0:T(8,128)(2,1)S(1)}, u32[]{:S(2)}, u32[]{:S(2)}) collective-permute-start(bf16[16,128,128]{2,1,0:T(8,128)(2,1)S(1)} %get-tuple-element.45.mine), channel_id=1, source_target_pairs={{0,1},{1,0},{2,3},{3,2},{4,5},{5,4},{6,7},{7,6},{8,9},{9,8},{10,11... | collective-permute-start | bytes 1572872 | tf_op jit(solution)/shard_map/ppermute | solution.py:22
  35.1 14.3 %collective-permute-start.3 = (bf16[16,128,128]{2,1,0:T(8,128)(2,1)S(1)}, bf16[16,128,128]{2,1,0:T(8,128)(2,1)S(1)}, u32[]{:S(2)}, u32[]{:S(2)}) collective-permute-start(bf16[16,128,128]{2,1,0:T(8,128)(2,1)S(1)} %get-tuple-element.49), channel_id=1, source_target_pairs={{0,2},{1,3},{2,0},{3,1},{4,6},{5,7},{6,4},{7,5},{8,10},{9,11},{10,... | collective-permute-start | bytes 1572872 | tf_op jit(solution)/shard_map/ppermute | solution.py:22
  47.4 3.4 %copy-start.5 = (f32[8192]{0:T(1024)S(1)}, f32[8192]{0:T(1024)}, u32[]{:S(2)}) copy-start(f32[8192]{0:T(1024)} %param.12) | copy-start | bytes 98308
  50.8 1.9 %collective-permute-start.4 = (bf16[16,128,128]{2,1,0:T(8,128)(2,1)S(1)}, bf16[16,128,128]{2,1,0:T(8,128)(2,1)S(1)}, u32[]{:S(2)}, u32[]{:S(2)}) collective-permute-start(bf16[16,128,128]{2,1,0:T(8,128)(2,1)S(1)} %get-tuple-element.48.mine), channel_id=1, source_target_pairs={{0,1},{1,0},{2,3},{3,2},{4,5},{5,4},{6,7},{7,6},{8,9},{9,8},{10,11... | collective-permute-start | bytes 1572872 | tf_op jit(solution)/shard_map/ppermute | solution.py:22
  52.7 10.0 %copy-start.4 = (f32[16,128,128]{2,1,0:T(8,128)S(1)}, f32[16,128,128]{2,1,0:T(8,128)}, u32[]{:S(2)}) copy-start(f32[16,128,128]{2,1,0:T(8,128)} %get-tuple-element.35) | copy-start | bytes 3145732
  62.6 14.9 %collective-permute-start.6 = (bf16[16,128,128]{2,1,0:T(8,128)(2,1)S(1)}, bf16[16,128,128]{2,1,0:T(8,128)(2,1)S(1)}, u32[]{:S(2)}, u32[]{:S(2)}) collective-permute-start(bf16[16,128,128]{2,1,0:T(8,128)(2,1)S(1)} %get-tuple-element.38), channel_id=1, source_target_pairs={{0,4},{4,0},{8,12},{12,8},{16,20},{20,16},{24,28},{28,24},{1,5},{5... | collective-permute-start | bytes 1572872 | tf_op jit(solution)/shard_map/ppermute | solution.py:22
  62.6 13.0 %collective-permute-start.9 = (bf16[16,128,128]{2,1,0:T(8,128)(2,1)S(1)}, bf16[16,128,128]{2,1,0:T(8,128)(2,1)S(1)}, u32[]{:S(2)}, u32[]{:S(2)}) collective-permute-start(bf16[16,128,128]{2,1,0:T(8,128)(2,1)S(1)} %get-tuple-element.40), channel_id=1, source_target_pairs={{0,8},{4,12},{8,0},{12,4},{16,24},{20,28},{24,16},{28,20},{1,9},{5... | collective-permute-start | bytes 1572872 | tf_op jit(solution)/shard_map/ppermute | solution.py:22
  63.8 1.3 collective-permute-start.5
  75.7 6.4 %collective-permute-start.10 = (bf16[8,128,128]{2,1,0:T(8,128)(2,1)S(1)}, bf16[8,128,128]{2,1,0:T(8,128)(2,1)S(1)}, u32[]{:S(2)}, u32[]{:S(2)}) collective-permute-start(bf16[8,128,128]{2,1,0:T(8,128)(2,1)S(1)} %reduce-precision_convert_fusion.5), channel_id=1, source_target_pairs={{0,4},{4,0},{8,12},{12,8},{16,20},{20,16},{24,28},{28,24},{1,5},{5... | collective-permute-start | bytes 786440 | tf_op jit(solution)/shard_map/ppermute | solution.py:22
  77.5 10.8 %copy-start.3 = (f32[16,128,128]{2,1,0:T(8,128)S(1)}, f32[16,128,128]{2,1,0:T(8,128)}, u32[]{:S(2)}) copy-start(f32[16,128,128]{2,1,0:T(8,128)} %copy-done.2) | copy-start | bytes 3145732
  77.6 8.9 %collective-permute-start.7 = (bf16[10,128,128]{2,1,0:T(8,128)(2,1)S(1)}, bf16[10,128,128]{2,1,0:T(8,128)(2,1)S(1)}, u32[]{:S(2)}, u32[]{:S(2)}) collective-permute-start(bf16[10,128,128]{2,1,0:T(8,128)(2,1)S(1)} %pad_maximum_fusion.2), channel_id=1, source_target_pairs={{0,8},{4,12},{8,0},{12,4},{16,24},{20,28},{24,16},{28,20},{1,9},{5... | collective-permute-start | bytes 983048 | tf_op jit(solution)/shard_map/ppermute | solution.py:22
  82.3 23.6 %collective-permute-start.11 = (bf16[8,128,128]{2,1,0:T(8,128)(2,1)S(1)}, bf16[8,128,128]{2,1,0:T(8,128)(2,1)S(1)}, u32[]{:S(2)}, u32[]{:S(2)}) collective-permute-start(bf16[8,128,128]{2,1,0:T(8,128)(2,1)S(1)} %reduce-precision_convert_fusion.4), channel_id=1, source_target_pairs={{0,16},{4,20},{8,24},{12,28},{16,0},{20,4},{24,8},{28,12},{1,17},{... | collective-permute-start | bytes 786440 | tf_op jit(solution)/shard_map/ppermute | solution.py:22
  86.7 25.1 %collective-permute-start.8 = (bf16[10,128,128]{2,1,0:T(8,128)(2,1)S(1)}, bf16[10,128,128]{2,1,0:T(8,128)(2,1)S(1)}, u32[]{:S(2)}, u32[]{:S(2)}) collective-permute-start(bf16[10,128,128]{2,1,0:T(8,128)(2,1)S(1)} %pad_maximum_fusion.3), channel_id=1, source_target_pairs={{0,16},{4,20},{8,24},{12,28},{16,0},{20,4},{24,8},{28,12},{1,17},{... | collective-permute-start | bytes 983048 | tf_op jit(solution)/shard_map/ppermute | solution.py:22
  112.0 7.3 %collective-permute-start.13 = (bf16[8,128,128]{2,1,0:T(8,128)(2,1)S(1)}, bf16[8,128,128]{2,1,0:T(8,128)(2,1)S(1)}, u32[]{:S(2)}, u32[]{:S(2)}) collective-permute-start(bf16[8,128,128]{2,1,0:T(8,128)(2,1)S(1)} %multiply_convert_fusion.2), channel_id=1, source_target_pairs={{0,8},{4,12},{8,0},{12,4},{16,24},{20,28},{24,16},{28,20},{1,9},{5... | collective-permute-start | bytes 786440 | tf_op jit(solution)/shard_map/ppermute | solution.py:22
  112.8 10.7 %collective-permute-start.12 = (bf16[10,128,128]{2,1,0:T(8,128)(2,1)S(1)}, bf16[10,128,128]{2,1,0:T(8,128)(2,1)S(1)}, u32[]{:S(2)}, u32[]{:S(2)}) collective-permute-start(bf16[10,128,128]{2,1,0:T(8,128)(2,1)S(1)} %pad_maximum_fusion.4), channel_id=1, source_target_pairs={{0,4},{4,0},{8,12},{12,8},{16,20},{20,16},{24,28},{28,24},{1,5},{5... | collective-permute-start | bytes 983048 | tf_op jit(solution)/shard_map/ppermute | solution.py:22
  119.4 17.3 %collective-permute-start.14 = (bf16[16,128,128]{2,1,0:T(8,128)(2,1)S(1)}, bf16[16,128,128]{2,1,0:T(8,128)(2,1)S(1)}, u32[]{:S(2)}, u32[]{:S(2)}) collective-permute-start(bf16[16,128,128]{2,1,0:T(8,128)(2,1)S(1)} %maximum_select_fusion.2), channel_id=1, source_target_pairs={{0,4},{4,0},{8,12},{12,8},{16,20},{20,16},{24,28},{28,24},{1,5},{5... | collective-permute-start | bytes 1572872 | tf_op jit(solution)/shard_map/ppermute | solution.py:22
  123.6 13.3 %collective-permute-start.15 = (bf16[16,128,128]{2,1,0:T(8,128)(2,1)S(1)}, bf16[16,128,128]{2,1,0:T(8,128)(2,1)S(1)}, u32[]{:S(2)}, u32[]{:S(2)}) collective-permute-start(bf16[16,128,128]{2,1,0:T(8,128)(2,1)S(1)} %maximum_select_fusion.3), channel_id=1, source_target_pairs={{0,8},{4,12},{8,0},{12,4},{16,24},{20,28},{24,16},{28,20},{1,9},{5... | collective-permute-start | bytes 1572872 | tf_op jit(solution)/shard_map/ppermute | solution.py:22

commit v4 on v3

--- a/solution.py
+++ b/solution.py
@@ -458,15 +458,14 @@
 def reduce_rest(own, arrived, bits, extra=None):
     parts = [own, arrived]
     for i, bit in enumerate(bits[1:]):
-        last = i == len(bits) - 2
-        if last:
+        if i == len(bits) - 2:
             give = rounded(sum(x.astype(F32) for x in parts))
             parts = [give]
         else:
             split = [halves(x, bit_of("img", bit)) for x in parts]
             give = rounded(sum(x.astype(F32) for _, x in split))
             parts = [x for x, _ in split]
-        if extra is None:
+        if extra is None or i > 0:
             arrived = swap(give, "img", bit)
         else:
             arrived, extra = swap_with(give, extra, "img", bit)
@@ -565,7 +564,10 @@
     got_a = swap(send_a, "img", order_a[0])
     got_b = swap(send_b, "img", order_b[0])
     gram = gram + products(image_two)
-    gram = in_two(gram + swap(gram, "cap", 0))
+    gram = gram + swap(gram, "cap", 0)
+    for bit in range(2, img_bits):
+        gram = gram + swap(gram, "img", bit)
+    gram = in_two(gram)
     sum_a, gram = reduce_rest(own_a, got_a, order_a, gram)
     sum_b, _ = reduce_rest(own_b, got_b, order_b)
     next_a = (sum_a * scatter_start(scale_a, order_a)).astype(BF16)

time: 141 us -> 140 us (level)
  the two profiles are of different devices: /device:TPU:0 before, /device:TPU:18 now
where the time goes in v4:
time: 140 us; the launch traced here: 138 us
  waiting for transfers between devices  57.7 us (41%)
  Pallas kernels  49.3 us (35%)
  starting transfers between devices  19 us (14%)
  other arithmetic  5.82 us (4%)
  matrix products  4.46 us (3%)
  between operations  1.65 us (1%)
    ppermute x17, waiting for transfers between devices, swap(): lax.ppermute(row_major(x), axis, [(i, i ^ 1 << bit) for i in range(n)])  57.7 us
    ppermute x17, starting transfers between devices, swap(): lax.ppermute(row_major(x), axis, [(i, i ^ 1 << bit) for i in range(n)])  19 us
    pallas_call x1, Pallas kernels, forward(): pl.pallas_call(functools.partial(image_kernel, shares, cut), in_specs=[SM...  16.2 us
    pallas_call x1, Pallas kernels, backward_two(): pl.pallas_call(fourth_kernel, in_specs=[SMEM, SMEM, HBM, VMEM, ANY, ANY],...  11.3 us
    pallas_call x1, Pallas kernels, backward_one(): pl.pallas_call(third_kernel, in_specs=[SMEM, HBM, ANY, ANY], out_specs=[V...  10 us
    pallas_call x1, Pallas kernels, factorize(): pl.pallas_call(functools.partial(factor_kernel, root), in_specs=[VMEM], o...  9.97 us
  transfers between devices with their start and end apart: 17, of which 12 were waited for; matrix products, arithmetic and copies ran while one was open for 5% of the time, Pallas kernels for 16%

profile of v4, /device:TPU:18, one launch (start us, length us, event | category | flops | bytes accessed | tf_op | source)
XLA Modules:
  0.0 138.4 jit_solution(7934254550247622749)
XLA Ops:
  1.4 16.2 %image.1 = (f32[16,128,128]{2,1,0:T(8,128)S(1)}, f32[16,128,128]{2,1,0:T(8,128)S(1)}, bf16[32,128,128]{2,1,0:T(8,128)(2,1)S(1)}) custom-call(s32[2]{0:T(128)S(1)} %pad_add_fusion.meta, s32[1,640]{1,0:T(1,128)} %rows.1, s32[1,640]{1,0:T(1,128)} %cols.1, f32[64,128]{1,0:T(8,128)} %bitcast.63, bf16[64,128,128]{2,1,0:T(8,128)(2,1)} %bitcast.62, ...), custom_call_target="tpu_custom_call" | custom-call | tf_op jit(solution)/shard_map/image/pallas_call | solution.py:328
  17.7 2.6 %collective-permute-done = bf16[32,128,128]{2,1,0:T(8,128)(2,1)S(1)} collective-permute-done((bf16[32,128,128]{2,1,0:T(8,128)(2,1)S(1)}, bf16[32,128,128]{2,1,0:T(8,128)(2,1)S(1)}, u32[]{:S(2)}, u32[]{:S(2)}) %collective-permute-start) | collective-permute-done | bytes 1048608 | tf_op jit(solution)/shard_map/ppermute | solution.py:22
  20.7 0.3 copy-done
  21.0 1.8 %orders.1 = (s32[8,768]{1,0:T(8,128)S(1)}, s32[8,768]{1,0:T(8,128)S(1)}) custom-call(s32[2]{0:T(128)S(1)} %pad_add_fusion.meta, s32[1,640]{1,0:T(1,128)S(1)} %copy-done, s32[1,640]{1,0:T(1,128)S(1)} %copy-done.1), custom_call_target="tpu_custom_call" | custom-call | tf_op jit(solution)/shard_map/orders/pallas_call | solution.py:357
  22.9 11.7 %collective-permute-done.1 = bf16[16,128,128]{2,1,0:T(8,128)(2,1)S(1)} collective-permute-done((bf16[16,128,128]{2,1,0:T(8,128)(2,1)S(1)}, bf16[16,128,128]{2,1,0:T(8,128)(2,1)S(1)}, u32[]{:S(2)}, u32[]{:S(2)}) %collective-permute-start.1) | collective-permute-done | bytes 524320 | tf_op jit(solution)/shard_map/ppermute | solution.py:22
  34.6 0.4 multiply_convert_fusion.1
  35.1 0.4 collective-permute-start.3
  35.4 1.0 convolution_bitcast_fusion.1
  36.5 0.5 collective-permute-done.2.other
  37.0 10.0 %caption_one.1 = (bf16[64,128,128]{2,1,0:T(8,128)(2,1)S(1)}, f32[1,128]{1,0:T(1,128)S(1)}) custom-call(s32[8,768]{1,0:T(8,128)S(1)} %get-tuple-element.28.order, bf16[640,128,128]{2,1,0:T(8,128)(2,1)} %tiles.5, bf16[16,128,128]{2,1,0:T(8,128)(2,1)S(1)} %get-tuple-element.45.mine, bf16[16,128,128]{2,1,0:T(8,128)(2,1)S(1)} %collective-permute-done.2.other), custom_call_target="tpu_custom_call" | custom-call | tf_op jit(solution)/shard_map/caption_one/pallas_call | solution.py:370
  47.1 2.3 %collective-permute-done.3 = bf16[16,128,128]{2,1,0:T(8,128)(2,1)S(1)} collective-permute-done((bf16[16,128,128]{2,1,0:T(8,128)(2,1)S(1)}, bf16[16,128,128]{2,1,0:T(8,128)(2,1)S(1)}, u32[]{:S(2)}, u32[]{:S(2)}) %collective-permute-start.3) | collective-permute-done | bytes 524320 | tf_op jit(solution)/shard_map/ppermute | solution.py:22
  49.4 1.3 add_multiply_fusion
  50.9 1.8 %collective-permute-done.4.other = bf16[16,128,128]{2,1,0:T(8,128)(2,1)S(1)} collective-permute-done((bf16[16,128,128]{2,1,0:T(8,128)(2,1)S(1)}, bf16[16,128,128]{2,1,0:T(8,128)(2,1)S(1)}, u32[]{:S(2)}, u32[]{:S(2)}) %collective-permute-start.4) | collective-permute-done | bytes 524320 | tf_op jit(solution)/shard_map/ppermute | solution.py:22
  52.7 11.3 %caption_two.1 = (f32[16,128,128]{2,1,0:T(8,128)S(1)}, bf16[16,128,128]{2,1,0:T(8,128)(2,1)S(1)}, f32[16,128,128]{2,1,0:T(8,128)S(1)}, bf16[16,128,128]{2,1,0:T(8,128)(2,1)S(1)}) custom-call(s32[2]{0:T(128)S(1)} %pad_add_fusion.1.meta, s32[8,768]{1,0:T(8,128)S(1)} %get-tuple-element.27.order, bf16[640,128,128]{2,1,0:T(8,128)(2,1)} %tiles.5, ...), custom_call_target="tpu_custom_call" | custom-call | tf_op jit(solution)/shard_map/caption_two/pallas_call | solution.py:394
  64.1 1.0 fusion
  65.2 2.1 %collective-permute-start.7 = (bf16[16,128,128]{2,1,0:T(8,128)(2,1)S(1)}, bf16[16,128,128]{2,1,0:T(8,128)(2,1)S(1)}, u32[]{:S(2)}, u32[]{:S(2)}) collective-permute-start(bf16[16,128,128]{2,1,0:T(8,128)(2,1)S(1)} %get-tuple-element.38), channel_id=1, source_target_pairs={{0,4},{4,0},{8,12},{12,8},{16,20},{20,16},{24,28},{28,24},{1,5},{5... | collective-permute-start | bytes 1572872 | tf_op jit(solution)/shard_map/ppermute | solution.py:22
  67.4 8.0 %collective-permute-done.6 = f32[128,128]{1,0:T(8,128)S(1)} collective-permute-done((f32[128,128]{1,0:T(8,128)S(1)}, f32[128,128]{1,0:T(8,128)S(1)}, u32[]{:S(2)}, u32[]{:S(2)}) %collective-permute-start.6) | collective-permute-done | bytes 65568 | tf_op jit(solution)/shard_map/ppermute | solution.py:22
  75.4 4.1 %collective-permute-start.10 = (bf16[8,128,128]{2,1,0:T(8,128)(2,1)S(1)}, bf16[8,128,128]{2,1,0:T(8,128)(2,1)S(1)}, u32[]{:S(2)}, u32[]{:S(2)}) collective-permute-start(bf16[8,128,128]{2,1,0:T(8,128)(2,1)S(1)} %reduce-precision_convert_fusion.6), channel_id=1, source_target_pairs={{0,4},{4,0},{8,12},{12,8},{16,20},{20,16},{24,28},{28,24},{1,5},{5... | collective-permute-start | bytes 786440 | tf_op jit(solution)/shard_map/ppermute | solution.py:22
  79.9 2.3 %collective-permute-start.8 = (bf16[10,128,128]{2,1,0:T(8,128)(2,1)S(1)}, bf16[10,128,128]{2,1,0:T(8,128)(2,1)S(1)}, u32[]{:S(2)}, u32[]{:S(2)}) collective-permute-start(bf16[10,128,128]{2,1,0:T(8,128)(2,1)S(1)} %pad_maximum_fusion.2), channel_id=1, source_target_pairs={{0,8},{4,12},{8,0},{12,4},{16,24},{20,28},{24,16},{28,20},{1,9},{5... | collective-permute-start | bytes 983048 | tf_op jit(solution)/shard_map/ppermute | solution.py:22
  82.3 3.8 %collective-permute-done.10 = bf16[8,128,128]{2,1,0:T(8,128)(2,1)S(1)} collective-permute-done((bf16[8,128,128]{2,1,0:T(8,128)(2,1)S(1)}, bf16[8,128,128]{2,1,0:T(8,128)(2,1)S(1)}, u32[]{:S(2)}, u32[]{:S(2)}) %collective-permute-start.10) | collective-permute-done | bytes 262176 | tf_op jit(solution)/shard_map/ppermute | solution.py:22
  86.4 4.4 %collective-permute-done.8 = bf16[10,128,128]{2,1,0:T(8,128)(2,1)S(1)} collective-permute-done((bf16[10,128,128]{2,1,0:T(8,128)(2,1)S(1)}, bf16[10,128,128]{2,1,0:T(8,128)(2,1)S(1)}, u32[]{:S(2)}, u32[]{:S(2)}) %collective-permute-start.8) | collective-permute-done | bytes 327712 | tf_op jit(solution)/shard_map/ppermute | solution.py:22
  91.1 13.3 %collective-permute-done.11 = bf16[8,128,128]{2,1,0:T(8,128)(2,1)S(1)} collective-permute-done((bf16[8,128,128]{2,1,0:T(8,128)(2,1)S(1)}, bf16[8,128,128]{2,1,0:T(8,128)(2,1)S(1)}, u32[]{:S(2)}, u32[]{:S(2)}) %collective-permute-start.11) | collective-permute-done | bytes 262176 | tf_op jit(solution)/shard_map/ppermute | solution.py:22
  104.6 1.7 %collective-permute-start.12 = (bf16[10,128,128]{2,1,0:T(8,128)(2,1)S(1)}, bf16[10,128,128]{2,1,0:T(8,128)(2,1)S(1)}, u32[]{:S(2)}, u32[]{:S(2)}) collective-permute-start(bf16[10,128,128]{2,1,0:T(8,128)(2,1)S(1)} %pad_maximum_fusion.3), channel_id=1, source_target_pairs={{0,4},{4,0},{8,12},{12,8},{16,20},{20,16},{24,28},{28,24},{1,5},{5... | collective-permute-start | bytes 983048 | tf_op jit(solution)/shard_map/ppermute | solution.py:22
  106.3 2.6 %collective-permute-done.13 = bf16[8,128,128]{2,1,0:T(8,128)(2,1)S(1)} collective-permute-done((bf16[8,128,128]{2,1,0:T(8,128)(2,1)S(1)}, bf16[8,128,128]{2,1,0:T(8,128)(2,1)S(1)}, u32[]{:S(2)}, u32[]{:S(2)}) %collective-permute-start.13) | collective-permute-done | bytes 262176 | tf_op jit(solution)/shard_map/ppermute | solution.py:22
  109.1 4.5 %collective-permute-start.14 = (bf16[8,128,128]{2,1,0:T(8,128)(2,1)S(1)}, bf16[8,128,128]{2,1,0:T(8,128)(2,1)S(1)}, u32[]{:S(2)}, u32[]{:S(2)}) collective-permute-start(bf16[8,128,128]{2,1,0:T(8,128)(2,1)S(1)} %multiply_convert_fusion.2), channel_id=1, source_target_pairs={{0,8},{4,12},{8,0},{12,4},{16,24},{20,28},{24,16},{28,20},{1,9},{5... | collective-permute-start | bytes 786440 | tf_op jit(solution)/shard_map/ppermute | solution.py:22
  113.7 6.4 %collective-permute-done.14 = bf16[8,128,128]{2,1,0:T(8,128)(2,1)S(1)} collective-permute-done((bf16[8,128,128]{2,1,0:T(8,128)(2,1)S(1)}, bf16[8,128,128]{2,1,0:T(8,128)(2,1)S(1)}, u32[]{:S(2)}, u32[]{:S(2)}) %collective-permute-start.14) | collective-permute-done | bytes 262176 | tf_op jit(solution)/shard_map/ppermute | solution.py:22
  120.1 1.5 %collective-permute-start.15 = (bf16[16,128,128]{2,1,0:T(8,128)(2,1)S(1)}, bf16[16,128,128]{2,1,0:T(8,128)(2,1)S(1)}, u32[]{:S(2)}, u32[]{:S(2)}) collective-permute-start(bf16[16,128,128]{2,1,0:T(8,128)(2,1)S(1)} %maximum_select_fusion.2), channel_id=1, source_target_pairs={{0,4},{4,0},{8,12},{12,8},{16,20},{20,16},{24,28},{28,24},{1,5},{5... | collective-permute-start | bytes 1572872 | tf_op jit(solution)/shard_map/ppermute | solution.py:22
  121.8 1.8 %collective-permute-start.16 = (bf16[16,128,128]{2,1,0:T(8,128)(2,1)S(1)}, bf16[16,128,128]{2,1,0:T(8,128)(2,1)S(1)}, u32[]{:S(2)}, u32[]{:S(2)}) collective-permute-start(bf16[16,128,128]{2,1,0:T(8,128)(2,1)S(1)} %maximum_select_fusion.3), channel_id=1, source_target_pairs={{0,8},{4,12},{8,0},{12,4},{16,24},{20,28},{24,16},{28,20},{1,9},{5... | collective-permute-start | bytes 1572872 | tf_op jit(solution)/shard_map/ppermute | solution.py:22
  123.6 0.7 convert_add_fusion.gram
  124.2 10.0 %factorize.1 = (f32[128,128]{1,0:T(8,128)}, f32[128,128]{1,0:T(8,128)}) custom-call(f32[128,128]{1,0:T(8,128)} %convert_add_fusion.gram), custom_call_target="tpu_custom_call" | custom-call | tf_op jit(solution)/shard_map/factorize/pallas_call | solution.py:417
  134.2 2.4 %fusion.14 = f32[2048,128]{1,0:T(8,128)} fusion(f32[2048,128]{1,0:T(8,128)S(1)} %bitcast.60, f32[128,128]{1,0:T(8,128)} %get-tuple-element.41), kind=kOutput, calls=%fused_computation.56 | convolution fusion | flops 201326592 | bytes 2162688 | tf_op jit(solution)/shard_map/dot_general | solution.py:586
  136.9 1.5 %pad_maximum_fusion = bf16[64,128,128]{2,1,0:T(8,128)(2,1)} fusion(bf16[32,128,128]{2,1,0:T(8,128)(2,1)S(1)} %maximum_select_fusion.1, bf16[32,128,128]{2,1,0:T(8,128)(2,1)S(1)} %maximum_select_fusion), kind=kLoop, calls=%fused_computation | loop fusion | flops 1048576 | bytes 4194304 | tf_op jit(solution)/shard_map/concatenate | solution.py:577
  (59 shorter events, 3.1 us)
Async XLA Ops:
  17.6 2.7 %collective-permute-start = (bf16[32,128,128]{2,1,0:T(8,128)(2,1)S(1)}, bf16[32,128,128]{2,1,0:T(8,128)(2,1)S(1)}, u32[]{:S(2)}, u32[]{:S(2)}) collective-permute-start(bf16[32,128,128]{2,1,0:T(8,128)(2,1)S(1)} %get-tuple-element.24), channel_id=1, source_target_pairs={{0,1},{1,0},{2,3},{3,2},{4,5},{5,4},{6,7},{7,6},{8,9},{9,8},{10,11... | collective-permute-start | bytes 3145736 | tf_op jit(solution)/shard_map/ppermute | solution.py:22
  20.3 0.7 copy-start
  20.3 0.7 copy-start.1
  20.3 2.5 %copy-start.6 = (f32[8192]{0:T(1024)S(1)}, f32[8192]{0:T(1024)}, u32[]{:S(2)}) copy-start(f32[8192]{0:T(1024)} %param.11) | copy-start | bytes 98308
  20.6 14.0 %collective-permute-start.1 = (bf16[16,128,128]{2,1,0:T(8,128)(2,1)S(1)}, bf16[16,128,128]{2,1,0:T(8,128)(2,1)S(1)}, u32[]{:S(2)}, u32[]{:S(2)}) collective-permute-start(bf16[16,128,128]{2,1,0:T(8,128)(2,1)S(1)} %get-tuple-element.50), channel_id=1, source_target_pairs={{0,2},{1,3},{2,0},{3,1},{4,6},{5,7},{6,4},{7,5},{8,10},{9,11},{10,... | collective-permute-start | bytes 1572872 | tf_op jit(solution)/shard_map/ppermute | solution.py:22
  35.0 12.0 %copy-start.3 = (f32[16,128,128]{2,1,0:T(8,128)}, f32[16,128,128]{2,1,0:T(8,128)S(1)}, u32[]{:S(2)}) copy-start(f32[16,128,128]{2,1,0:T(8,128)S(1)} %get-tuple-element.46) | copy-start | bytes 3145732
  35.0 2.0 %collective-permute-start.2 = (bf16[16,128,128]{2,1,0:T(8,128)(2,1)S(1)}, bf16[16,128,128]{2,1,0:T(8,128)(2,1)S(1)}, u32[]{:S(2)}, u32[]{:S(2)}) collective-permute-start(bf16[16,128,128]{2,1,0:T(8,128)(2,1)S(1)} %get-tuple-element.45.mine), channel_id=1, source_target_pairs={{0,1},{1,0},{2,3},{3,2},{4,5},{5,4},{6,7},{7,6},{8,9},{9,8},{10,11... | collective-permute-start | bytes 1572872 | tf_op jit(solution)/shard_map/ppermute | solution.py:22
  35.1 14.3 %collective-permute-start.3 = (bf16[16,128,128]{2,1,0:T(8,128)(2,1)S(1)}, bf16[16,128,128]{2,1,0:T(8,128)(2,1)S(1)}, u32[]{:S(2)}, u32[]{:S(2)}) collective-permute-start(bf16[16,128,128]{2,1,0:T(8,128)(2,1)S(1)} %get-tuple-element.49), channel_id=1, source_target_pairs={{0,2},{1,3},{2,0},{3,1},{4,6},{5,7},{6,4},{7,5},{8,10},{9,11},{10,... | collective-permute-start | bytes 1572872 | tf_op jit(solution)/shard_map/ppermute | solution.py:22
  47.0 3.7 %copy-start.5 = (f32[8192]{0:T(1024)S(1)}, f32[8192]{0:T(1024)}, u32[]{:S(2)}) copy-start(f32[8192]{0:T(1024)} %param.12) | copy-start | bytes 98308
  50.8 1.9 %collective-permute-start.4 = (bf16[16,128,128]{2,1,0:T(8,128)(2,1)S(1)}, bf16[16,128,128]{2,1,0:T(8,128)(2,1)S(1)}, u32[]{:S(2)}, u32[]{:S(2)}) collective-permute-start(bf16[16,128,128]{2,1,0:T(8,128)(2,1)S(1)} %get-tuple-element.48.mine), channel_id=1, source_target_pairs={{0,1},{1,0},{2,3},{3,2},{4,5},{5,4},{6,7},{7,6},{8,9},{9,8},{10,11... | collective-permute-start | bytes 1572872 | tf_op jit(solution)/shard_map/ppermute | solution.py:22
  52.7 11.4 %copy-start.2 = (f32[16,128,128]{2,1,0:T(8,128)S(1)}, f32[16,128,128]{2,1,0:T(8,128)}, u32[]{:S(2)}) copy-start(f32[16,128,128]{2,1,0:T(8,128)} %get-tuple-element.35) | copy-start | bytes 3145732
  64.0 11.4 %collective-permute-start.9 = (bf16[16,128,128]{2,1,0:T(8,128)(2,1)S(1)}, bf16[16,128,128]{2,1,0:T(8,128)(2,1)S(1)}, u32[]{:S(2)}, u32[]{:S(2)}) collective-permute-start(bf16[16,128,128]{2,1,0:T(8,128)(2,1)S(1)} %get-tuple-element.40), channel_id=1, source_target_pairs={{0,8},{4,12},{8,0},{12,4},{16,24},{20,28},{24,16},{28,20},{1,9},{5... | collective-permute-start | bytes 1572872 | tf_op jit(solution)/shard_map/ppermute | solution.py:22
  65.1 17.2 %copy-start.4 = (f32[16,128,128]{2,1,0:T(8,128)S(1)}, f32[16,128,128]{2,1,0:T(8,128)}, u32[]{:S(2)}) copy-start(f32[16,128,128]{2,1,0:T(8,128)} %copy-done.3) | copy-start | bytes 3145732
  65.1 2.2 %collective-permute-start.5 = (f32[128,128]{1,0:T(8,128)S(1)}, f32[128,128]{1,0:T(8,128)S(1)}, u32[]{:S(2)}, u32[]{:S(2)}) collective-permute-start(f32[128,128]{1,0:T(8,128)S(1)} %fusion), channel_id=1, source_target_pairs={{0,1},{1,0},{2,3},{3,2},{4,5},{5,4},{6,7},{7,6},{8,9},{9,8},{10,11... | collective-permute-start | bytes 196616 | tf_op jit(solution)/shard_map/ppermute | solution.py:22
  65.2 14.6 %collective-permute-start.7 = (bf16[16,128,128]{2,1,0:T(8,128)(2,1)S(1)}, bf16[16,128,128]{2,1,0:T(8,128)(2,1)S(1)}, u32[]{:S(2)}, u32[]{:S(2)}) collective-permute-start(bf16[16,128,128]{2,1,0:T(8,128)(2,1)S(1)} %get-tuple-element.38), channel_id=1, source_target_pairs={{0,4},{4,0},{8,12},{12,8},{16,20},{20,16},{24,28},{28,24},{1,5},{5... | collective-permute-start | bytes 1572872 | tf_op jit(solution)/shard_map/ppermute | solution.py:22
  67.3 8.1 %collective-permute-start.6 = (f32[128,128]{1,0:T(8,128)S(1)}, f32[128,128]{1,0:T(8,128)S(1)}, u32[]{:S(2)}, u32[]{:S(2)}) collective-permute-start(f32[128,128]{1,0:T(8,128)S(1)} %add.126), channel_id=1, source_target_pairs={{0,16},{4,20},{8,24},{12,28},{16,0},{20,4},{24,8},{28,12},{1,17},{... | collective-permute-start | bytes 196616 | tf_op jit(solution)/shard_map/ppermute | solution.py:22
  75.4 10.6 %collective-permute-start.10 = (bf16[8,128,128]{2,1,0:T(8,128)(2,1)S(1)}, bf16[8,128,128]{2,1,0:T(8,128)(2,1)S(1)}, u32[]{:S(2)}, u32[]{:S(2)}) collective-permute-start(bf16[8,128,128]{2,1,0:T(8,128)(2,1)S(1)} %reduce-precision_convert_fusion.6), channel_id=1, source_target_pairs={{0,4},{4,0},{8,12},{12,8},{16,20},{20,16},{24,28},{28,24},{1,5},{5... | collective-permute-start | bytes 786440 | tf_op jit(solution)/shard_map/ppermute | solution.py:22
  79.9 10.9 %collective-permute-start.8 = (bf16[10,128,128]{2,1,0:T(8,128)(2,1)S(1)}, bf16[10,128,128]{2,1,0:T(8,128)(2,1)S(1)}, u32[]{:S(2)}, u32[]{:S(2)}) collective-permute-start(bf16[10,128,128]{2,1,0:T(8,128)(2,1)S(1)} %pad_maximum_fusion.2), channel_id=1, source_target_pairs={{0,8},{4,12},{8,0},{12,4},{16,24},{20,28},{24,16},{28,20},{1,9},{5... | collective-permute-start | bytes 983048 | tf_op jit(solution)/shard_map/ppermute | solution.py:22
  86.2 18.1 %collective-permute-start.11 = (bf16[8,128,128]{2,1,0:T(8,128)(2,1)S(1)}, bf16[8,128,128]{2,1,0:T(8,128)(2,1)S(1)}, u32[]{:S(2)}, u32[]{:S(2)}) collective-permute-start(bf16[8,128,128]{2,1,0:T(8,128)(2,1)S(1)} %reduce-precision_convert_fusion.5), channel_id=1, source_target_pairs={{0,16},{4,20},{8,24},{12,28},{16,0},{20,4},{24,8},{28,12},{1,17},{... | collective-permute-start | bytes 786440 | tf_op jit(solution)/shard_map/ppermute | solution.py:22
  90.9 17.9 %collective-permute-start.13 = (bf16[8,128,128]{2,1,0:T(8,128)(2,1)S(1)}, bf16[8,128,128]{2,1,0:T(8,128)(2,1)S(1)}, u32[]{:S(2)}, u32[]{:S(2)}) collective-permute-start(bf16[8,128,128]{2,1,0:T(8,128)(2,1)S(1)} %reduce-precision_convert_fusion.4), channel_id=1, source_target_pairs={{0,16},{4,20},{8,24},{12,28},{16,0},{20,4},{24,8},{28,12},{1,17},{... | collective-permute-start | bytes 786440 | tf_op jit(solution)/shard_map/ppermute | solution.py:22
  104.6 17.0 %collective-permute-start.12 = (bf16[10,128,128]{2,1,0:T(8,128)(2,1)S(1)}, bf16[10,128,128]{2,1,0:T(8,128)(2,1)S(1)}, u32[]{:S(2)}, u32[]{:S(2)}) collective-permute-start(bf16[10,128,128]{2,1,0:T(8,128)(2,1)S(1)} %pad_maximum_fusion.3), channel_id=1, source_target_pairs={{0,4},{4,0},{8,12},{12,8},{16,20},{20,16},{24,28},{28,24},{1,5},{5... | collective-permute-start | bytes 983048 | tf_op jit(solution)/shard_map/ppermute | solution.py:22
  109.1 11.0 %collective-permute-start.14 = (bf16[8,128,128]{2,1,0:T(8,128)(2,1)S(1)}, bf16[8,128,128]{2,1,0:T(8,128)(2,1)S(1)}, u32[]{:S(2)}, u32[]{:S(2)}) collective-permute-start(bf16[8,128,128]{2,1,0:T(8,128)(2,1)S(1)} %multiply_convert_fusion.2), channel_id=1, source_target_pairs={{0,8},{4,12},{8,0},{12,4},{16,24},{20,28},{24,16},{28,20},{1,9},{5... | collective-permute-start | bytes 786440 | tf_op jit(solution)/shard_map/ppermute | solution.py:22
  120.1 16.4 %collective-permute-start.15 = (bf16[16,128,128]{2,1,0:T(8,128)(2,1)S(1)}, bf16[16,128,128]{2,1,0:T(8,128)(2,1)S(1)}, u32[]{:S(2)}, u32[]{:S(2)}) collective-permute-start(bf16[16,128,128]{2,1,0:T(8,128)(2,1)S(1)} %maximum_select_fusion.2), channel_id=1, source_target_pairs={{0,4},{4,0},{8,12},{12,8},{16,20},{20,16},{24,28},{28,24},{1,5},{5... | collective-permute-start | bytes 1572872 | tf_op jit(solution)/shard_map/ppermute | solution.py:22
  121.8 15.0 %collective-permute-start.16 = (bf16[16,128,128]{2,1,0:T(8,128)(2,1)S(1)}, bf16[16,128,128]{2,1,0:T(8,128)(2,1)S(1)}, u32[]{:S(2)}, u32[]{:S(2)}) collective-permute-start(bf16[16,128,128]{2,1,0:T(8,128)(2,1)S(1)} %maximum_select_fusion.3), channel_id=1, source_target_pairs={{0,8},{4,12},{8,0},{12,4},{16,24},{20,28},{24,16},{28,20},{1,9},{5... | collective-permute-start | bytes 1572872 | tf_op jit(solution)/shard_map/ppermute | solution.py:22
